TPU v7x, 32 devices: a whole 2x2x4 slice. The times are simulated.
32 devices in a mesh: dp: 2 (over y), fsdp: 16 (over z, x, core).
Axes of the slice: x: 2, y: 2, z: 4, core: 2. Of those that a mesh axis runs over, the one named last changes fastest.
Arguments:
- field_five: bfloat16 [192, 5, 5, 512], P(('dp', 'fsdp')), may hold values from -6 to 6
- field_seven: bfloat16 [64, 7, 7, 512], P(('dp', 'fsdp')), may hold values from -6 to 6
- field_nine: bfloat16 [64, 9, 9, 512], P(('dp', 'fsdp')), may hold values from -6 to 6
- mask_five: int32 [192, 5, 5], P(('dp', 'fsdp')), may hold values from 0 to 1, as said below
- mask_seven: int32 [64, 7, 7], P(('dp', 'fsdp')), may hold values from 0 to 1, as said below
- mask_nine: int32 [64, 9, 9], P(('dp', 'fsdp')), may hold values from 0 to 1, as said below
- back_five: bfloat16 [192, 5, 5, 512], P(('dp', 'fsdp')), may hold values from -6 to 6
- back_seven: bfloat16 [64, 7, 7, 512], P(('dp', 'fsdp')), may hold values from -6 to 6
- back_nine: bfloat16 [64, 9, 9, 512], P(('dp', 'fsdp')), may hold values from -6 to 6
- kernels: float32 [2, 3, 3, 512, 512], P(None, None, None, None, 'fsdp'), may hold values from -0.09375 to 0.09375
- norm_params: float32 [4, 512], P(None, 'fsdp'), may hold values from 0.4 to 1.6
- kernel_first: float32 [2, 3, 3, 512, 512], P(None, None, None, None, 'fsdp'), may hold values from -320 to 320
- kernel_second: float32 [2, 3, 3, 512, 512], P(None, None, None, None, 'fsdp'), may hold values from 2624 to 10496
- norm_first: float32 [4, 512], P(None, 'fsdp'), may hold values from -320 to 320
- norm_second: float32 [4, 512], P(None, 'fsdp'), may hold values from 2624 to 10496
Outputs:
- out_five: bfloat16 [192, 5, 5, 512], P(('dp', 'fsdp'))
- out_seven: bfloat16 [64, 7, 7, 512], P(('dp', 'fsdp'))
- out_nine: bfloat16 [64, 9, 9, 512], P(('dp', 'fsdp'))
- grad_five: float32 [192, 5, 5, 512], P(('dp', 'fsdp'))
- grad_seven: float32 [64, 7, 7, 512], P(('dp', 'fsdp'))
- grad_nine: float32 [64, 9, 9, 512], P(('dp', 'fsdp'))
- kernels_next: float32 [2, 3, 3, 512, 512], P(None, None, None, None, 'fsdp')
- kernel_first_next: float32 [2, 3, 3, 512, 512], P(None, None, None, None, 'fsdp')
- kernel_second_next: float32 [2, 3, 3, 512, 512], P(None, None, None, None, 'fsdp')
- norm_next: float32 [4, 512], P(None, 'fsdp')
- norm_first_next: float32 [4, 512], P(None, 'fsdp')
- norm_second_next: float32 [4, 512], P(None, 'fsdp')
Inputs may be any that keep to these rules, and one draw needn't show every extreme that they name: `mask_five`: 1 marks a valid pixel; the valid pixels of an image form a rectangle at its top-left corner, which may be empty. `mask_seven`: 1 marks a valid pixel; the valid pixels of an image form a rectangle at its top-left corner, which may be empty. `mask_nine`: 1 marks a valid pixel; the valid pixels of an image form a rectangle at its top-left corner, which may be empty.
All inputs are finite; a program needn't handle non-finite values.
Results may differ from a plain program's by a relative error of at most 0.0097.
Values may be sent and summed in bfloat16 or wider, within the bound.
No kernel may reach another device: no remote copies, remote signals or barrier semaphores. Data moves between devices by JAX's collectives and lax.ppermute only.
A program may use at most 128 MiB of HBM per device.

v0:
```python
import jax
import jax.numpy as jnp
from jax import lax
from jax.sharding import PartitionSpec as P

STEP = 5


NORM_EPS = 1e-05
BETA_ONE = 0.5
BETA_TWO = 0.5
KERNEL_RATE = 0.03
NORM_RATE = 0.4
KERNEL_DECAY = 0.01
ADAM_EPS = 1e-08


def swish(value):
    return value * jax.nn.sigmoid(value)


def swish_slope(value):
    logistic = jax.nn.sigmoid(value)
    return logistic * (1.0 + value * (1.0 - logistic))


def regroup(flat, shapes):
    pieces = []
    offset = 0
    for image_count, map_side in shapes:
        row_count = image_count * map_side * map_side
        pieces.append(
            flat[offset : offset + row_count].reshape(
                image_count, map_side, map_side, flat.shape[1]
            )
        )
        offset += row_count
    return pieces


def convolve(flat, kernel, shapes):
    results = []
    for images in regroup(flat, shapes):
        mapped = lax.conv_general_dilated(
            images,
            kernel,
            (1, 1),
            ((1, 1), (1, 1)),
            dimension_numbers=("NHWC", "HWIO", "NHWC"),
            preferred_element_type=jnp.float32,
        )
        results.append(mapped.reshape(-1, kernel.shape[3]))
    return jnp.concatenate(results, axis=0)


def flipped(kernel):
    return jnp.transpose(kernel[::-1, ::-1], (0, 1, 3, 2))


def kernel_grad(flat_in, flat_grad, shapes):
    summed = None
    for images_in, images_grad in zip(regroup(flat_in, shapes), regroup(flat_grad, shapes)):
        term = lax.conv_general_dilated(
            images_in,
            images_grad,
            (1, 1),
            ((1, 1), (1, 1)),
            dimension_numbers=("CHWN", "IHWO", "NHWC"),
            preferred_element_type=jnp.float32,
        )
        summed = term if summed is None else summed + term
    return jnp.transpose(summed, (1, 2, 0, 3))


def statistics(hidden, valid, local_total):
    first_sum, total = lax.psum((jnp.sum(hidden * valid, axis=0), local_total), ("dp", "fsdp"))
    centre = first_sum / total
    spread = lax.psum(jnp.sum(jnp.square(hidden - centre) * valid, axis=0), ("dp", "fsdp")) / total
    return (centre, lax.rsqrt(spread + NORM_EPS), total)


def norm_back(grad_out, normed, inv_std, gain, valid, total):
    shift_grad, gain_grad = lax.psum(
        (jnp.sum(grad_out, axis=0), jnp.sum(grad_out * normed, axis=0)), ("dp", "fsdp")
    )
    grad_in = (
        valid * (gain * inv_std) * (grad_out - shift_grad / total - normed * gain_grad / total)
    )
    return (grad_in.astype(jnp.bfloat16), gain_grad, shift_grad)


def adamw(param, grad, first, second, rate, decay):
    first_new = BETA_ONE * first + (1.0 - BETA_ONE) * grad
    second_new = BETA_TWO * second + (1.0 - BETA_TWO) * grad * grad
    first_hat = first_new / (1.0 - BETA_ONE**STEP)
    second_hat = second_new / (1.0 - BETA_TWO**STEP)
    update = first_hat / (jnp.sqrt(second_hat) + ADAM_EPS)
    return (param - rate * (update + decay * param), first_new, second_new)


def local(
    field_five,
    field_seven,
    field_nine,
    mask_five,
    mask_seven,
    mask_nine,
    back_five,
    back_seven,
    back_nine,
    kernels,
    norm_params,
    kernel_first,
    kernel_second,
    norm_first,
    norm_second,
):
    fields = (field_five, field_seven, field_nine)
    masks = (mask_five, mask_seven, mask_nine)
    backs = (back_five, back_seven, back_nine)
    channels = field_five.shape[3]
    shapes = [(field.shape[0], field.shape[1]) for field in fields]
    inputs = jnp.concatenate([field.reshape(-1, channels) for field in fields], axis=0)
    valid = jnp.concatenate([mask.reshape(-1) for mask in masks]).astype(jnp.float32)[:, None]
    residual = inputs.astype(jnp.float32)
    source = inputs * valid.astype(jnp.bfloat16)
    kernel_low = kernels.astype(jnp.bfloat16)
    full_kernels, full_norm = (
        lax.all_gather(kernel_low, "fsdp", axis=4, tiled=True),
        lax.all_gather(norm_params.astype(jnp.bfloat16), "fsdp", axis=1, tiled=True),
    )
    gains = full_norm.astype(jnp.float32)
    local_total = jnp.sum(valid)
    first_out = convolve(source, full_kernels[0], shapes)
    centre_one, inv_one, total = statistics(first_out, valid, local_total)
    normed_one = (first_out - centre_one) * inv_one
    hidden_one = normed_one * gains[0] + gains[1]
    active = (swish(hidden_one) * valid).astype(jnp.bfloat16)
    second_out = convolve(active, full_kernels[1], shapes)
    centre_two, inv_two, total = statistics(second_out, valid, local_total)
    normed_two = (second_out - centre_two) * inv_two
    summed = normed_two * gains[2] + gains[3] + residual
    result = (swish(summed) * valid).astype(jnp.bfloat16)
    grad_back = jnp.concatenate(
        [cotangent.reshape(-1, channels) for cotangent in backs], axis=0
    ).astype(jnp.float32)
    grad_sum = grad_back * valid * swish_slope(summed)
    grad_two, gain_two, shift_two = norm_back(grad_sum, normed_two, inv_two, gains[2], valid, total)
    back_kernels = lax.all_gather(kernel_low, "fsdp", axis=4, tiled=True)
    grad_active = convolve(grad_two, flipped(back_kernels[1]), shapes)
    grad_hidden = grad_active * valid * swish_slope(hidden_one)
    grad_one, gain_one, shift_one = norm_back(
        grad_hidden, normed_one, inv_one, gains[0], valid, total
    )
    grad_source = convolve(grad_one, flipped(back_kernels[0]), shapes)
    grad_input = grad_sum + valid * grad_source
    kernel_grads = jnp.stack(
        [kernel_grad(source, grad_one, shapes), kernel_grad(active, grad_two, shapes)]
    )
    owned = lax.psum_scatter(kernel_grads, "fsdp", scatter_dimension=4, tiled=True)
    owned = lax.psum(owned, "dp")
    norm_full = jnp.stack([gain_one, shift_one, gain_two, shift_two])
    shard_width = norm_params.shape[1]
    norm_grads = lax.dynamic_slice_in_dim(
        norm_full, lax.axis_index("fsdp") * shard_width, shard_width, 1
    )
    kernels_next, kernel_first_next, kernel_second_next = adamw(
        kernels, owned, kernel_first, kernel_second, KERNEL_RATE, KERNEL_DECAY
    )
    norm_next, norm_first_next, norm_second_next = adamw(
        norm_params, norm_grads, norm_first, norm_second, NORM_RATE, 0.0
    )
    out_groups = regroup(result, shapes)
    grad_groups = regroup(grad_input, shapes)
    return (
        out_groups[0],
        out_groups[1],
        out_groups[2],
        grad_groups[0],
        grad_groups[1],
        grad_groups[2],
        kernels_next,
        kernel_first_next,
        kernel_second_next,
        norm_next,
        norm_first_next,
        norm_second_next,
    )


def solution(mesh):
    in_specs = (
        P(("dp", "fsdp"), None, None, None),
        P(("dp", "fsdp"), None, None, None),
        P(("dp", "fsdp"), None, None, None),
        P(("dp", "fsdp"), None, None),
        P(("dp", "fsdp"), None, None),
        P(("dp", "fsdp"), None, None),
        P(("dp", "fsdp"), None, None, None),
        P(("dp", "fsdp"), None, None, None),
        P(("dp", "fsdp"), None, None, None),
        P(None, None, None, None, "fsdp"),
        P(None, "fsdp"),
        P(None, None, None, None, "fsdp"),
        P(None, None, None, None, "fsdp"),
        P(None, "fsdp"),
        P(None, "fsdp"),
    )
    out_specs = (
        P(("dp", "fsdp"), None, None, None),
        P(("dp", "fsdp"), None, None, None),
        P(("dp", "fsdp"), None, None, None),
        P(("dp", "fsdp"), None, None, None),
        P(("dp", "fsdp"), None, None, None),
        P(("dp", "fsdp"), None, None, None),
        P(None, None, None, None, "fsdp"),
        P(None, None, None, None, "fsdp"),
        P(None, None, None, None, "fsdp"),
        P(None, "fsdp"),
        P(None, "fsdp"),
        P(None, "fsdp"),
    )
    return jax.shard_map(local, mesh=mesh, in_specs=in_specs, out_specs=out_specs, check_vma=False)
```

profile of v0, /device:TPU:0, one launch (start us, length us, event | category | flops | bytes accessed | tf_op | source)
XLA Modules:
  0.0 910.5 jit_solution(9417643127988836883)
XLA Ops:
  7.3 3.1 copy.279
  10.5 0.7 copy.171
  11.3 0.7 copy.172
  12.2 0.7 copy.170
  13.2 0.9 copy.168
  14.1 1.0 copy.167
  15.2 1.0 copy.169
  16.6 23.3 %all-gather = bf16[16,32,4]{1,2,0:T(4,128)(2,1)S(1)} all-gather(bf16[1,32,4]{1,2,0:T(4,128)(2,1)S(1)} %convert_bitcast_fusion), channel_id=1, replica_groups=mesh['dp'=2,'fsdp'=16] {'fsdp'}, dimensions={0}, use_global_device_ids=true | all-gather | bytes 4352 | tf_op jit(solution)/shard_map/all_gather | solution.py:130
  40.6 0.7 fusion.59
  41.3 53.9 %all-gather.3.cloned.1.call-done = bf16[2,3,3,512,512]{3,0,2,1,4:T(2,128)(2,1)} async-done(((bf16[2,3,3,512,32]{3,0,2,1,4:T(2,128)(2,1)}), bf16[2,3,3,512,512]{3,0,2,1,4:T(2,128)(2,1)}) %all-gather.3.cloned.1.call-update) | async-done | bytes 9437200 | tf_op jit(solution)/shard_map/all_gather | solution.py:129
  95.1 19.6 %fusion.68 = (bf16[1,3,3,512,512]{3,0,2,1,4:T(2,128)(2,1)}, bf16[1,3,3,512,512]{3,0,2,1,4:T(2,128)(2,1)}) fusion(bf16[2,3,3,512,512]{3,0,2,1,4:T(2,128)(2,1)} %all-gather.3.cloned.1.call-done), kind=kLoop, calls=%fused_computation.113 | loop fusion | bytes 18874368 | tf_op jit(solution)/shard_map/slice | solution.py:134
  114.7 22.2 %copy.227 = bf16[1,3,3,512,512]{4,3,2,1,0:T(8,128)(2,1)} copy(bf16[1,3,3,512,512]{3,0,2,1,4:T(2,128)(2,1)} %get-tuple-element.84) | data formatting | bytes 9437184
  136.9 4.1 fusion.20
  141.1 5.0 fusion.18
  146.2 3.9 fusion.22
  150.6 38.6 %all-reduce.3 = (f32[512]{0:T(512)S(1)}, f32[]{:T(128)}) all-reduce(f32[512]{0:T(512)S(1)} %multiply_reduce_fusion.5, f32[]{:T(128)} %fusion.59), channel_id=1, replica_groups=mesh['dp'=2,'fsdp'=16] {'dp','fsdp'}, use_global_device_ids=true, to_apply=%region_1.0 | all-reduce | flops 513 | bytes 4104 | tf_op jit(solution)/shard_map/psum | solution.py:76
  189.2 0.6 broadcast_divide_fusion.3
  190.0 41.6 %psum.75 = f32[512]{0:T(512)S(1)} all-reduce(f32[512]{0:T(512)S(1)} %multiply_reduce_fusion.4), channel_id=1, replica_groups=mesh['dp'=2,'fsdp'=16] {'dp','fsdp'}, use_global_device_ids=true, to_apply=%region_5.0 | all-reduce | flops 512 | bytes 4096 | tf_op jit(solution)/shard_map/psum | solution.py:78
  231.6 0.7 fusion.64
  232.3 0.3 multiply_convert_fusion.3
  232.9 22.3 %copy.228 = bf16[1,3,3,512,512]{4,3,2,1,0:T(8,128)(2,1)} copy(bf16[1,3,3,512,512]{3,0,2,1,4:T(2,128)(2,1)} %get-tuple-element.85) | data formatting | bytes 9437184
  255.3 4.1 fusion.8
  259.4 5.0 fusion.6
  264.6 4.1 fusion.10
  269.1 39.1 %psum.76 = f32[512]{0:T(512)S(1)} all-reduce(f32[512]{0:T(512)S(1)} %multiply_reduce_fusion.3), channel_id=1, replica_groups=mesh['dp'=2,'fsdp'=16] {'dp','fsdp'}, use_global_device_ids=true, to_apply=%region_7.0 | all-reduce | flops 512 | bytes 4096 | tf_op jit(solution)/shard_map/psum | solution.py:76
  308.2 0.6 broadcast_divide_fusion.2
  309.0 40.9 %psum.77 = f32[512]{0:T(512)S(1)} all-reduce(f32[512]{0:T(512)S(1)} %multiply_reduce_fusion.2), channel_id=1, replica_groups=mesh['dp'=2,'fsdp'=16] {'dp','fsdp'}, use_global_device_ids=true, to_apply=%region_9.0 | all-reduce | flops 512 | bytes 4096 | tf_op jit(solution)/shard_map/psum | solution.py:78
  350.0 0.7 fusion.66
  350.6 0.7 fusion.61
  351.3 39.3 %all-reduce.2 = (f32[512]{0:T(512)S(1)}, f32[512]{0:T(512)S(1)}) all-reduce(f32[512]{0:T(512)S(1)} %get-tuple-element.63, f32[512]{0:T(512)S(1)} %get-tuple-element.62), channel_id=1, replica_groups=mesh['dp'=2,'fsdp'=16] {'dp','fsdp'}, use_global_device_ids=true, to_apply=%region_13.0 | all-reduce | flops 1024 | bytes 8192 | tf_op jit(solution)/shard_map/psum | solution.py:83
  390.6 0.7 broadcast_divide_fusion.1
  391.3 2.0 multiply_convert_fusion.1
  393.6 4.5 fusion.2
  398.2 5.2 fusion
  403.5 1.9 fusion.4
  405.9 0.6 fusion.60
  406.4 41.1 %all-reduce.1 = (f32[512]{0:T(512)S(1)}, f32[512]{0:T(512)S(1)}) all-reduce(f32[512]{0:T(512)S(1)} %get-tuple-element.61, f32[512]{0:T(512)S(1)} %get-tuple-element.60), channel_id=1, replica_groups=mesh['dp'=2,'fsdp'=16] {'dp','fsdp'}, use_global_device_ids=true, to_apply=%region_17.0 | all-reduce | flops 1024 | bytes 8192 | tf_op jit(solution)/shard_map/psum | solution.py:83
  447.6 0.7 broadcast_divide_fusion
  448.3 0.9 multiply_convert_fusion
  449.3 7.2 fusion.48
  456.6 5.2 fusion.38
  462.1 6.3 fusion.45
  468.4 5.3 fusion.35
  473.7 5.8 add_bitcast_fusion
  479.6 8.7 add_bitcast_fusion.1
  488.4 7.8 pad_maximum_fusion
  496.1 28.5 %copy.219 = f32[2,3,3,512,512]{3,0,2,1,4:T(2,128)} copy(f32[2,3,3,512,512]{4,3,2,1,0:T(8,128)} %pad_maximum_fusion) | data formatting | bytes 37748736 | tf_op jit(solution)/shard_map/stack | solution.py:157
  524.7 0.6 copy-done.36
  525.2 0.6 dynamic-slice
  526.5 4.4 fusion.14
  530.9 322.1 %all-reduce.9.cloned.1.call-done = f32[2,3,3,512,512]{3,0,2,1,4:T(2,128)} async-done(((f32[2,3,3,512,512]{3,0,2,1,4:T(2,128)}), f32[2,3,3,512,512]{3,0,2,1,4:T(2,128)}) %all-reduce.9.cloned.1.call-update) | async-done | bytes 18874384
  853.0 1.7 constant_dynamic-slice_fusion
  854.6 1.2 copy.220
  855.9 4.3 fusion.16
  860.7 5.5 fusion.12
  866.7 0.7 copy.222
  867.5 0.7 copy.221
  868.4 0.8 copy.223
  869.2 0.8 copy.225
  870.1 0.9 copy.224
  871.1 1.0 copy.226
  872.1 0.7 multiply_subtract_fusion.1
  872.8 26.2 %all-reduce.7.cloned.1.call-done = f32[2,3,3,512,32]{3,4,2,1,0:T(8,128)} async-done(((f32[2,3,3,512,32]{3,4,2,1,0:T(8,128)}), f32[2,3,3,512,32]{3,4,2,1,0:T(8,128)}) %all-reduce.7.cloned.1.call-update) | async-done | bytes 1179664 | tf_op jit(solution)/shard_map/psum | solution.py:161
  899.1 4.5 multiply_subtract_fusion
  (177 shorter events, 5.8 us)
Async XLA Ops:
  7.2 9.4 %copy-start.28 = (f32[4,32]{1,0:T(4,128)S(1)}, f32[4,32]{1,0:T(4,128)}, u32[]{:S(2)}) copy-start(f32[4,32]{1,0:T(4,128)} %param.25) | copy-start | bytes 1540
  7.2 32.8 %copy-start.23 = (bf16[2,7,7,512]{3,0,2,1:T(2,128)(2,1)S(1)}, bf16[2,7,7,512]{3,0,2,1:T(2,128)(2,1)}, u32[]{:S(2)}) copy-start(bf16[2,7,7,512]{3,0,2,1:T(2,128)(2,1)} %param.22) | copy-start | bytes 301060
  7.2 32.9 %copy-start.15 = (bf16[6,5,5,512]{3,0,2,1:T(8,128)(2,1)S(1)}, bf16[6,5,5,512]{3,0,2,1:T(8,128)(2,1)}, u32[]{:S(2)}) copy-start(bf16[6,5,5,512]{3,0,2,1:T(8,128)(2,1)} %param.21) | copy-start | bytes 460804
  7.2 33.0 %copy-start.16 = (bf16[2,9,9,512]{3,0,2,1:T(2,128)(2,1)S(1)}, bf16[2,9,9,512]{3,0,2,1:T(2,128)(2,1)}, u32[]{:S(2)}) copy-start(bf16[2,9,9,512]{3,0,2,1:T(2,128)(2,1)} %param.23) | copy-start | bytes 497668
  7.2 87.9 %all-gather.3.cloned.1.call-start = ((), (), s32[]{:S(2)}) async-start(), calls=%async_computation | async-start | bytes 10027008 | tf_op jit(solution)/shard_map/all_gather | solution.py:129
  10.4 842.6 %all-reduce.9.cloned.1.call-start = ((), (), s32[]{:S(2)}) async-start(), calls=%async_computation.2 | async-start | bytes 37748736
  16.3 431.9 %copy-start.13 = (f32[410]{0:T(512)}, f32[410]{0:T(512)S(1)}, u32[]{:S(2)}) copy-start(f32[410]{0:T(512)S(1)} %get-tuple-element.83) | copy-start | bytes 4924
  40.4 96.5 %copy-start.17 = (bf16[2,7,7,512]{3,2,1,0:T(8,128)(2,1)}, bf16[2,7,7,512]{3,2,1,0:T(8,128)(2,1)S(1)}, u32[]{:S(2)}) copy-start(bf16[2,7,7,512]{3,2,1,0:T(8,128)(2,1)S(1)} %reshape.233) | copy-start | bytes 301060
  40.5 105.7 %copy-start = (bf16[6,5,5,512]{3,2,1,0:T(8,128)(2,1)}, bf16[6,5,5,512]{3,2,1,0:T(8,128)(2,1)S(1)}, u32[]{:S(2)}) copy-start(bf16[6,5,5,512]{3,2,1,0:T(8,128)(2,1)S(1)} %reshape.231) | copy-start | bytes 460804
  40.6 100.5 %copy-start.8 = (bf16[2,9,9,512]{3,2,1,0:T(8,128)(2,1)}, bf16[2,9,9,512]{3,2,1,0:T(8,128)(2,1)S(1)}, u32[]{:S(2)}) copy-start(bf16[2,9,9,512]{3,2,1,0:T(8,128)(2,1)S(1)} %reshape.235) | copy-start | bytes 497668
  232.7 22.5 %copy-start.19 = (bf16[2,7,7,512]{3,2,1,0:T(8,128)(2,1)}, bf16[2,7,7,512]{3,2,1,0:T(8,128)(2,1)S(1)}, u32[]{:S(2)}) copy-start(bf16[2,7,7,512]{3,2,1,0:T(8,128)(2,1)S(1)} %reshape.239) | copy-start | bytes 301060
  232.8 31.8 %copy-start.2 = (bf16[6,5,5,512]{3,2,1,0:T(8,128)(2,1)}, bf16[6,5,5,512]{3,2,1,0:T(8,128)(2,1)S(1)}, u32[]{:S(2)}) copy-start(bf16[6,5,5,512]{3,2,1,0:T(8,128)(2,1)S(1)} %reshape.237) | copy-start | bytes 460804
  232.9 26.5 %copy-start.10 = (bf16[2,9,9,512]{3,2,1,0:T(8,128)(2,1)}, bf16[2,9,9,512]{3,2,1,0:T(8,128)(2,1)S(1)}, u32[]{:S(2)}) copy-start(bf16[2,9,9,512]{3,2,1,0:T(8,128)(2,1)S(1)} %reshape.241) | copy-start | bytes 497668
  351.3 46.8 %copy-start.4 = (f32[410,512]{1,0:T(8,128)}, f32[410,512]{1,0:T(8,128)S(1)}, u32[]{:S(2)}) copy-start(f32[410,512]{1,0:T(8,128)S(1)} %get-tuple-element.81) | copy-start | bytes 2519044
  390.6 2.8 copy-start.24
  390.6 2.8 copy-start.30
  393.4 4.7 copy-start.21
  393.6 9.9 %copy-start.11 = (bf16[2,9,9,512]{3,2,1,0:T(8,128)(2,1)}, bf16[2,9,9,512]{3,2,1,0:T(8,128)(2,1)S(1)}, u32[]{:S(2)}) copy-start(bf16[2,9,9,512]{3,2,1,0:T(8,128)(2,1)S(1)} %reshape.253) | copy-start | bytes 497668
  398.1 5.4 slice-start
  398.2 5.3 slice-start.1
  405.7 43.6 %copy-start.12 = (bf16[2,9,9,512]{3,2,1,0:T(8,128)(2,1)S(1)}, bf16[2,9,9,512]{3,2,1,0:T(8,128)(2,1)}, u32[]{:S(2)}) copy-start(bf16[2,9,9,512]{3,2,1,0:T(8,128)(2,1)} %copy-done.11) | copy-start | bytes 497668
  447.6 9.0 copy-start.26
  447.6 9.0 copy-start.32
  449.3 7.3 copy-start.20
  449.3 7.3 copy-start.22
  456.6 5.5 copy-start.9
  456.6 17.1 %slice-start.2 = ((s8[9437184]{0:T(1024)(128)(4,1)}), s8[1048576]{0:T(1024)(128)(4,1)S(1)}, s32[]{:S(2)}) async-start(s8[9437184]{0:T(1024)(128)(4,1)} %bitcast.48), calls=%async_computation.5 | async-start | bytes 2097152
  462.0 6.4 copy-start.18
  462.1 11.6 %slice-start.3 = ((s8[9437184]{0:T(1024)(128)(4,1)}), s8[4194304]{0:T(1024)(128)(4,1)S(1)}, s32[]{:S(2)}) async-start(s8[9437184]{0:T(1024)(128)(4,1)} %bitcast.48), calls=%async_computation.6 | async-start | bytes 8388608
  462.1 11.6 %slice-start.4 = ((s8[9437184]{0:T(1024)(128)(4,1)}), s8[4194304]{0:T(1024)(128)(4,1)S(1)}, s32[]{:S(2)}) async-start(s8[9437184]{0:T(1024)(128)(4,1)} %bitcast.48), calls=%async_computation.7 | async-start | bytes 8388608
  468.4 5.3 copy-start.3
  473.7 5.9 copy-start.1
  524.6 0.7 copy-start.36
  524.6 374.4 %all-reduce.7.cloned.1.call-start = ((), (), s32[]{:S(2)}) async-start(), calls=%async_computation.1 | async-start | bytes 2359296 | tf_op jit(solution)/shard_map/psum | solution.py:161
  855.9 4.3 copy-start.7
  860.6 5.7 copy-start.5
  860.7 5.7 copy-start.14
  866.5 5.6 copy-start.25
  866.5 5.6 copy-start.27
  866.5 5.6 copy-start.29
  866.5 5.6 copy-start.31
  866.6 5.6 copy-start.33
  866.6 5.6 copy-start.34
  866.6 5.6 copy-start.35
  866.6 32.5 %copy-start.6 = (f32[2,3,3,512,32]{3,4,2,1,0:T(8,128)S(1)}, f32[2,3,3,512,32]{3,4,2,1,0:T(8,128)}, u32[]{:S(2)}) copy-start(f32[2,3,3,512,32]{3,4,2,1,0:T(8,128)} %param.24) | copy-start | bytes 3538948
Sparse Core Ops, SparseCore 0:
  10.9 84.1 all-gather.2
  524.7 328.1 all-reduce.8
  856.0 42.9 all-reduce.6
where the time goes:
time: 921 us; the launch traced here: 910 us
  waiting for transfers between devices  402 us (44%)
  blocking collectives  264 us (29%)
  local copies, waits for them, and re-layouts  114 us (12%)
  matrix products  90.6 us (10%)
  other arithmetic  22.9 us (2%)
  between operations  16.1 us (2%)
    unnamed x4, waiting for transfers between devices  322 us
    psum x2, blocking collectives, statistics(): lax.psum(jnp.sum(jnp.square(hidden - centre) * valid, axis=0), ('dp', 'fs...  82.5 us
    psum x2, blocking collectives, norm_back(): lax.psum((jnp.sum(grad_out, axis=0), jnp.sum(grad_out * normed, axis=0)),...  80.4 us
    psum x2, blocking collectives, statistics(): lax.psum((jnp.sum(hidden * valid, axis=0), local_total), ('dp', 'fsdp'))  77.8 us
    unnamed x104, local copies, waits for them, and re-layouts  60.8 us
    all_gather x1, waiting for transfers between devices, local(): lax.all_gather(kernel_low, 'fsdp', axis=4, tiled=True)  53.9 us
    conv_general_dilated x12, matrix products, convolve(): lax.conv_general_dilated(images, kernel, (1, 1), ((1, 1), (1, 1)), dimens...  51.9 us
    conv_general_dilated x6, matrix products, kernel_grad(): lax.conv_general_dilated(images_in, images_grad, (1, 1), ((1, 1), (1, 1))...  38.7 us
  transfers between devices with their start and end apart: 3, of which 3 were waited for; matrix products, arithmetic and copies ran while one was open for 3% of the time, Pallas kernels for 0%

commit v1 on v0

v1 whole, which is shorter than its diff:
```python
import functools

import jax
import jax.numpy as jnp
from jax import lax
from jax.experimental import pallas as pl
from jax.experimental.pallas import tpu as pltpu
from jax.sharding import PartitionSpec as P

STEP = 5
NORM_EPS = 1e-05
BETA_ONE = 0.5
BETA_TWO = 0.5
KERNEL_RATE = 0.03
NORM_RATE = 0.4
KERNEL_DECAY = 0.01
ADAM_EPS = 1e-08
AXES = ("dp", "fsdp")
TAPS = 9
LANES = 128
VMEM_BYTES = 56 * 1024 * 1024


def round_up(value, step):
    return (value + step - 1) // step * step


class Geometry:
    def __init__(self, shapes):
        self.shapes = shapes
        self.groups = []
        row, offset = 0, 0
        for count, side in shapes:
            down, right = (side + 1) * count, count
            rows = round_up(side * down, 8)
            halo = round_up(down + right, 8)
            offset = offset + halo
            self.groups.append((row, rows, offset, down, right))
            row += rows
            offset += rows + halo
        self.rows = row
        self.padded_rows = offset

    def flatten(self, arrays):
        pieces = []
        for array, (count, side), (_, rows, _, down, _) in zip(arrays, self.shapes, self.groups):
            moved = jnp.transpose(array, (1, 2, 0, 3))
            moved = jnp.pad(moved, ((0, 0), (0, 1), (0, 0), (0, 0)))
            moved = moved.reshape(side * down, array.shape[3])
            pieces.append(jnp.pad(moved, ((0, rows - side * down), (0, 0))))
        return jnp.concatenate(pieces, axis=0)

    def unflatten(self, flat):
        results = []
        for (count, side), (row, _, _, down, _) in zip(self.shapes, self.groups):
            piece = flat[row : row + side * down].reshape(side, side + 1, count, flat.shape[1])
            results.append(jnp.transpose(piece[:, :side], (2, 0, 1, 3)))
        return results

    def place(self, buffer, value):
        buffer[...] = jnp.zeros_like(buffer)
        for row, rows, offset, _, _ in self.groups:
            buffer[offset : offset + rows, :] = value[row : row + rows]

    def shifted(self, buffer, tap, sign):
        pieces = []
        for _, rows, offset, down, right in self.groups:
            start = offset + sign * ((tap // 3 - 1) * down + (tap % 3 - 1) * right)
            pieces.append(buffer[start : start + rows, :])
        return jnp.concatenate(pieces, axis=0).astype(jnp.bfloat16)


def wide(mask_ref, channels):
    return jnp.concatenate([mask_ref[...]] * (channels // LANES), axis=1)


def fetch(weight_hbm, weight_vmem, sems):
    copies = [
        pltpu.make_async_copy(weight_hbm.at[tap], weight_vmem.at[tap], sems.at[tap])
        for tap in range(TAPS)
    ]
    for copy in copies:
        copy.start()
    return copies


def multiply(left, right, left_dim, right_dim):
    return lax.dot_general(
        left, right, (((left_dim,), (right_dim,)), ((), ())), preferred_element_type=jnp.float32
    )


def column_sum(value):
    return jnp.sum(value, axis=0, keepdims=True)


def spread_rows(rows, ref):
    ref[...] = jnp.broadcast_to(jnp.concatenate(rows, axis=0)[None], ref.shape)


def local_statistics(hidden, valid, ref):
    count = column_sum(valid)
    total = column_sum(hidden * valid)
    centre = total / jnp.maximum(count, 1.0)
    squares = column_sum(jnp.square(hidden - centre) * valid)
    spread_rows([total, squares, count, centre], ref)


def global_statistics(gathered):
    totals, squares, counts, centres = (gathered[:, row, :] for row in range(4))
    total = column_sum(counts)
    centre = column_sum(totals) / total
    between = column_sum(counts * jnp.square(centres - centre))
    spread = (column_sum(squares) + between) / total
    return centre, lax.rsqrt(spread + NORM_EPS), total


def sigmoid(value):
    return 1.0 / (1.0 + jnp.exp(-value))


def swish_slope(value):
    logistic = sigmoid(value)
    return logistic * (1.0 + value * (1.0 - logistic))


def forward_one(geo, x_ref, mask_ref, weight_hbm, hidden_ref, stats_ref, buffer, weight, sems):
    copies = fetch(weight_hbm, weight, sems)
    valid = wide(mask_ref, x_ref.shape[1])
    geo.place(buffer, x_ref[...].astype(jnp.float32) * valid)
    for tap in range(TAPS):
        part = geo.shifted(buffer, tap, 1)
        copies[tap].wait()
        product = multiply(part, weight[tap], 1, 1)
        hidden_ref[...] = product if tap == 0 else hidden_ref[...] + product
    local_statistics(hidden_ref[...], valid, stats_ref)


def forward_two(
    geo,
    hidden_ref,
    gathered_ref,
    param_ref,
    mask_ref,
    weight_hbm,
    active_ref,
    second_ref,
    norm_ref,
    stats_ref,
    buffer,
    weight,
    sems,
):
    copies = fetch(weight_hbm, weight, sems)
    valid = wide(mask_ref, hidden_ref.shape[1])
    centre, inv, total = global_statistics(gathered_ref)
    norm_ref[...] = jnp.concatenate([centre, inv, total, total], axis=0)
    value = (hidden_ref[...] - centre) * inv * param_ref[0:1, :] + param_ref[1:2, :]
    active = value * sigmoid(value) * valid
    active_ref[...] = active.astype(jnp.bfloat16)
    geo.place(buffer, active)
    for tap in range(TAPS):
        part = geo.shifted(buffer, tap, 1)
        copies[tap].wait()
        product = multiply(part, weight[tap], 1, 1)
        second_ref[...] = product if tap == 0 else second_ref[...] + product
    local_statistics(second_ref[...], valid, stats_ref)


def turn(
    second_ref,
    gathered_ref,
    param_ref,
    mask_ref,
    x_ref,
    back_ref,
    result_ref,
    grad_ref,
    norm_ref,
    stats_ref,
):
    valid = wide(mask_ref, second_ref.shape[1])
    centre, inv, total = global_statistics(gathered_ref)
    norm_ref[...] = jnp.concatenate([centre, inv, total, total], axis=0)
    normed = (second_ref[...] - centre) * inv
    summed = normed * param_ref[2:3, :] + param_ref[3:4, :] + x_ref[...].astype(jnp.float32)
    logistic = sigmoid(summed)
    result_ref[...] = (summed * logistic * valid).astype(jnp.bfloat16)
    slope = logistic * (1.0 + summed * (1.0 - logistic))
    grad = back_ref[...].astype(jnp.float32) * valid * slope
    grad_ref[...] = grad
    spread_rows([column_sum(grad), column_sum(grad * normed)], stats_ref)


def norm_back(grad_ref, hidden_ref, norm_ref, gathered_ref, gain, valid, sums_ref):
    shift_grad = column_sum(gathered_ref[:, 0, :])
    gain_grad = column_sum(gathered_ref[:, 1, :])
    sums_ref[...] = jnp.concatenate([gain_grad, shift_grad], axis=0)
    centre, inv, total = norm_ref[0:1, :], norm_ref[1:2, :], norm_ref[2:3, :]
    normed = (hidden_ref[...] - centre) * inv
    grad = grad_ref[...] - shift_grad / total - normed * (gain_grad / total)
    return (valid * (gain * inv) * grad).astype(jnp.bfloat16)


def kernel_grad(geo, buffer, grad_in, out_ref):
    turned = jnp.transpose(grad_in.astype(jnp.float32)).astype(jnp.bfloat16)
    for tap in range(TAPS):
        product = multiply(turned, geo.shifted(buffer, tap, 1), 1, 0).astype(out_ref.dtype)
        if len(out_ref.shape) == 4:
            out_ref[:, tap, :, :] = product.reshape(
                out_ref.shape[0], out_ref.shape[2], out_ref.shape[3]
            )
        else:
            out_ref[tap] = product


def backward_two(
    geo,
    grad_ref,
    second_ref,
    norm_ref,
    gathered_ref,
    param_ref,
    mask_ref,
    active_ref,
    inner_ref,
    kernel_grad_ref,
    sums_ref,
    buffer,
):
    valid = wide(mask_ref, grad_ref.shape[1])
    inner = norm_back(
        grad_ref, second_ref, norm_ref, gathered_ref, param_ref[2:3, :], valid, sums_ref
    )
    inner_ref[...] = inner
    geo.place(buffer, active_ref[...].astype(jnp.float32))
    kernel_grad(geo, buffer, inner, kernel_grad_ref)


def backward_middle(
    geo,
    inner_ref,
    hidden_ref,
    norm_ref,
    param_ref,
    mask_ref,
    weight_hbm,
    grad_ref,
    stats_ref,
    buffer,
    weight,
    sems,
):
    copies = fetch(weight_hbm, weight, sems)
    valid = wide(mask_ref, hidden_ref.shape[1])
    geo.place(buffer, inner_ref[...].astype(jnp.float32))
    for tap in range(TAPS):
        part = geo.shifted(buffer, tap, -1)
        copies[tap].wait()
        product = multiply(part, weight[tap], 1, 0)
        grad_ref[...] = product if tap == 0 else grad_ref[...] + product
    normed = (hidden_ref[...] - norm_ref[0:1, :]) * norm_ref[1:2, :]
    value = normed * param_ref[0:1, :] + param_ref[1:2, :]
    grad = grad_ref[...] * valid * swish_slope(value)
    grad_ref[...] = grad
    spread_rows([column_sum(grad), column_sum(grad * normed)], stats_ref)


def backward_one(
    geo,
    grad_ref,
    hidden_ref,
    norm_ref,
    gathered_ref,
    param_ref,
    mask_ref,
    x_ref,
    inner_ref,
    kernel_grad_ref,
    sums_ref,
    buffer,
):
    valid = wide(mask_ref, grad_ref.shape[1])
    inner = norm_back(
        grad_ref, hidden_ref, norm_ref, gathered_ref, param_ref[0:1, :], valid, sums_ref
    )
    inner_ref[...] = inner
    geo.place(buffer, x_ref[...].astype(jnp.float32) * valid)
    kernel_grad(geo, buffer, inner, kernel_grad_ref)


def backward_input(
    geo, inner_ref, residual_ref, mask_ref, weight_hbm, grad_ref, buffer, weight, sems
):
    copies = fetch(weight_hbm, weight, sems)
    geo.place(buffer, inner_ref[...].astype(jnp.float32))
    for tap in range(TAPS):
        part = geo.shifted(buffer, tap, -1)
        copies[tap].wait()
        product = multiply(part, weight[tap], 1, 0)
        grad_ref[...] = product if tap == 0 else grad_ref[...] + product
    grad_ref[...] = residual_ref[...] + wide(mask_ref, grad_ref.shape[1]) * grad_ref[...]


def call(body, inputs, outputs, scratch=(), weights=()):
    whole = pl.BlockSpec(memory_space=pltpu.VMEM)
    return pl.pallas_call(
        body,
        out_shape=[jax.ShapeDtypeStruct(shape, dtype) for shape, dtype in outputs],
        in_specs=[whole] * len(inputs) + [pl.BlockSpec(memory_space=pl.ANY)] * len(weights),
        out_specs=[whole] * len(outputs),
        scratch_shapes=list(scratch),
        compiler_params=pltpu.CompilerParams(vmem_limit_bytes=VMEM_BYTES),
    )(*inputs, *weights)


def adamw(param, grad, first, second, rate, decay):
    first_new = BETA_ONE * first + (1.0 - BETA_ONE) * grad
    second_new = BETA_TWO * second + (1.0 - BETA_TWO) * grad * grad
    first_hat = first_new / (1.0 - BETA_ONE**STEP)
    second_hat = second_new / (1.0 - BETA_TWO**STEP)
    update = first_hat / (jnp.sqrt(second_hat) + ADAM_EPS)
    return (param - rate * (update + decay * param), first_new, second_new)


def exchange(spread):
    return lax.all_to_all(spread, AXES, 0, 0, tiled=True)


def local(
    devices,
    field_five,
    field_seven,
    field_nine,
    mask_five,
    mask_seven,
    mask_nine,
    back_five,
    back_seven,
    back_nine,
    kernels,
    norm_params,
    kernel_first,
    kernel_second,
    norm_first,
    norm_second,
):
    copies, shards = devices
    fields = (field_five, field_seven, field_nine)
    masks = (mask_five, mask_seven, mask_nine)
    backs = (back_five, back_seven, back_nine)
    channels = field_five.shape[3]
    width = kernels.shape[4]
    geo = Geometry([(field.shape[0], field.shape[1]) for field in fields])
    rows = geo.rows
    count = copies * shards
    f32, bf16 = jnp.float32, jnp.bfloat16

    def turned(kernel):
        return jnp.transpose(kernel, (0, 1, 2, 4, 3)).reshape(2, TAPS, width, channels)

    kernels_turned = turned(kernels)
    low = kernels_turned.astype(bf16)
    weight_one = lax.all_gather(low[0], "fsdp", axis=1, tiled=True)
    weight_two = lax.all_gather(low[1], "fsdp", axis=1, tiled=True)
    param_spread = jnp.broadcast_to(
        norm_params.astype(bf16).astype(f32)[None], (shards, 4, width)
    )
    params = lax.all_to_all(param_spread, "fsdp", 0, 0, tiled=True)
    params = jnp.transpose(params, (1, 0, 2)).reshape(4, channels)

    x = geo.flatten(fields)
    back = geo.flatten(backs)
    mask = geo.flatten([mask.astype(f32)[..., None] for mask in masks])
    mask = jnp.broadcast_to(mask, (rows, LANES))

    buffer = pltpu.VMEM((geo.padded_rows, channels), f32)
    weighted = (
        buffer,
        pltpu.VMEM((TAPS, channels, channels), bf16),
        pltpu.SemaphoreType.DMA((TAPS,)),
    )
    flat32 = ((rows, channels), f32)
    flat16 = ((rows, channels), bf16)
    four = ((count, 4, channels), f32)
    two = ((count, 2, channels), f32)
    norm = ((4, channels), f32)
    sums = ((2, channels), f32)
    if width % 16 == 0:
        grad_shape = ((shards, TAPS, width, channels), bf16)
    else:
        grad_shape = ((TAPS, channels, channels), bf16)

    def bind(body):
        return functools.partial(body, geo)

    hidden, stats = call(bind(forward_one), (x, mask), (flat32, four), weighted, (weight_one,))
    gathered = exchange(stats)
    active, second, norm_one, stats = call(
        bind(forward_two),
        (hidden, gathered, params, mask),
        (flat16, flat32, norm, four),
        weighted,
        (weight_two,),
    )
    gathered = exchange(stats)
    result, grad_sum, norm_two, stats = call(
        turn, (second, gathered, params, mask, x, back), (flat16, flat32, norm, two)
    )
    gathered = exchange(stats)
    inner_two, kernel_grad_two, sums_two = call(
        bind(backward_two),
        (grad_sum, second, norm_two, gathered, params, mask, active),
        (flat16, grad_shape, sums),
        (buffer,),
    )
    grad_hidden, stats = call(
        bind(backward_middle),
        (inner_two, hidden, norm_one, params, mask),
        (flat32, two),
        weighted,
        (weight_two,),
    )
    gathered = exchange(stats)
    inner_one, kernel_grad_one, sums_one = call(
        bind(backward_one),
        (grad_hidden, hidden, norm_one, gathered, params, mask, x),
        (flat16, grad_shape, sums),
        (buffer,),
    )
    (grad_input,) = call(
        bind(backward_input), (inner_one, grad_sum, mask), (flat32,), weighted, (weight_one,)
    )

    def reduced(value):
        if len(value.shape) == 3:
            value = jnp.transpose(
                value.reshape(TAPS, shards, width, channels), (1, 0, 2, 3)
            )
        owned = lax.psum_scatter(value, "fsdp", scatter_dimension=0, tiled=False)
        return lax.psum(owned, "dp").astype(f32)

    owned = jnp.stack([reduced(kernel_grad_one), reduced(kernel_grad_two)])
    results = adamw(
        kernels_turned,
        owned,
        turned(kernel_first),
        turned(kernel_second),
        KERNEL_RATE,
        KERNEL_DECAY,
    )
    kernel_results = [
        jnp.transpose(value.reshape(2, 3, 3, width, channels), (0, 1, 2, 4, 3))
        for value in results
    ]
    norm_full = jnp.concatenate([sums_one, sums_two], axis=0)
    norm_grads = lax.dynamic_slice_in_dim(norm_full, lax.axis_index("fsdp") * width, width, 1)
    norm_results = adamw(norm_params, norm_grads, norm_first, norm_second, NORM_RATE, 0.0)
    return (
        *geo.unflatten(result),
        *geo.unflatten(grad_input),
        *kernel_results,
        *norm_results,
    )


def solution(mesh):
    images = P(AXES, None, None, None)
    maps = P(AXES, None, None)
    weights = P(None, None, None, None, "fsdp")
    norms = P(None, "fsdp")
    in_specs = (
        (images,) * 3 + (maps,) * 3 + (images,) * 3 + (weights, norms, weights, weights, norms, norms)
    )
    out_specs = (images,) * 6 + (weights,) * 3 + (norms,) * 3
    body = functools.partial(local, (mesh.shape["dp"], mesh.shape["fsdp"]))
    return jax.shard_map(body, mesh=mesh, in_specs=in_specs, out_specs=out_specs, check_vma=False)
```

time: 921 us -> 365 us (0.40); the launches traced: 910 us -> 364 us
  blocking collectives: 264 us -> 23 us
  waiting for transfers between devices: 402 us -> 244 us
  local copies, waits for them, and re-layouts: 114 us -> 13.7 us
  matrix products: 90.6 us -> 0 us
  Pallas kernels: 0 us -> 45.9 us
  starting transfers between devices: 0.12 us -> 14.1 us
  other arithmetic: 22.9 us -> 8.96 us
    unnamed x4 -> x5, waiting for transfers between devices: 322 us -> 0.75 us
    psum x6 -> x0, blocking collectives: 241 us -> none  [the longest x2 82.5 us: statistics(): lax.psum(jnp.sum(jnp.square(hidden - centre) * valid, axis=0), ('dp', 'fs...]
    reduce_scatter x0 -> x2, waiting for transfers between devices: none -> 113 us  [reduced(): owned = lax.psum_scatter(value, 'fsdp', scatter_dimension=0, tiled=False)]
    conv_general_dilated x18 -> x0, matrix products: 90.6 us -> none  [the longest x12 51.9 us: convolve(): lax.conv_general_dilated(images, kernel, (1, 1), ((1, 1), (1, 1)), dimens...]
    unnamed x104 -> x43, local copies, waits for them, and re-layouts: 60.8 us -> 3.41 us
    pallas_call x0 -> x7, Pallas kernels: none -> 45.9 us  [call(): pl.pallas_call(body, out_shape=[jax.ShapeDtypeStruct(shape, dtype) for sh...]
    all_gather x1 -> x2, waiting for transfers between devices: 53.9 us -> 92.4 us  [the longest x1 46.3 us: local(): weight_two = lax.all_gather(low[1], 'fsdp', axis=1, tiled=True)]
    another operation x1 -> x0, local copies, waits for them, and re-layouts: 28.5 us -> none  [local(): jnp.stack([kernel_grad(source, grad_one, shapes), kernel_grad(active, gra...]
  transfers between devices with their start and end apart: 3 -> 8, of which waited for: 3 -> 6; matrix products, arithmetic and copies ran while one was open for 3% -> 4% of each run, Pallas kernels for 0% -> 8%
where the time goes in v1:
time: 365 us; the launch traced here: 364 us
  waiting for transfers between devices  244 us (67%)
  Pallas kernels  45.9 us (13%)
  blocking collectives  23 us (6%)
  between operations  14.3 us (4%)
  starting transfers between devices  14.1 us (4%)
  local copies, waits for them, and re-layouts  13.7 us (4%)
  other arithmetic  8.96 us (2%)
    reduce_scatter x2, waiting for transfers between devices, reduced(): owned = lax.psum_scatter(value, 'fsdp', scatter_dimension=0, tiled=False)  113 us
    all_gather x1, waiting for transfers between devices, local(): weight_two = lax.all_gather(low[1], 'fsdp', axis=1, tiled=True)  46.3 us
    all_gather x1, waiting for transfers between devices, local(): weight_one = lax.all_gather(low[0], 'fsdp', axis=1, tiled=True)  46.1 us
    pallas_call x7, Pallas kernels, call(): pl.pallas_call(body, out_shape=[jax.ShapeDtypeStruct(shape, dtype) for sh...  45.9 us
    psum x1, waiting for transfers between devices, reduced(): return lax.psum(owned, 'dp').astype(f32)  29 us
    all_to_all x2, blocking collectives, exchange(): return lax.all_to_all(spread, AXES, 0, 0, tiled=True)  23 us
    all_to_all x2, waiting for transfers between devices, exchange(): return lax.all_to_all(spread, AXES, 0, 0, tiled=True)  8.88 us
    all_to_all x1, starting transfers between devices, local(): params = lax.all_to_all(param_spread, 'fsdp', 0, 0, tiled=True)  7.36 us
  transfers between devices with their start and end apart: 8, of which 6 were waited for; matrix products, arithmetic and copies ran while one was open for 4% of the time, Pallas kernels for 8%

profile of v1, /device:TPU:0, one launch (start us, length us, event | category | flops | bytes accessed | tf_op | source)
XLA Modules:
  0.0 364.4 jit_solution(2764941425185512130)
XLA Ops:
  7.2 1.4 bitcast_convert_fusion
  8.6 0.9 fusion.20
  9.6 0.7 all-gather.5.cloned.1.call-update
  10.3 0.7 reshape.116
  11.0 7.4 %all-to-all-start.1 = ((f32[16,1,128]{2,1,0:T(1,128)}), f32[16,1,128]{2,1,0:T(1,128)S(1)}, u32[]{:S(2)}, u32[]{:S(2)}) async-start(f32[16,1,128]{2,1,0:T(1,128)} %reshape.116), calls=%async_computation.1 | async-start | bytes 16384 | tf_op jit(solution)/shard_map/all_to_all | solution.py:369
  18.4 0.1 pad.56
  18.5 0.1 reshape.100
  18.7 0.1 reshape.98
  18.8 0.1 pad.55
  18.8 0.1 reshape.99
  18.9 0.1 copy.38
  19.1 0.1 reshape.103
  19.2 0.1 copy.36
  19.4 0.1 reshape.101
  19.5 0.1 copy.37
  19.6 0.1 reshape.102
  19.8 0.8 fusion.11.x_ref
  20.6 0.1 fusion.16
  20.7 46.1 %all-gather.3.cloned.1.call-done.weight_hbm = bf16[9,512,512]{2,1,0:T(8,128)(2,1)} async-done(((bf16[9,32,512]{2,1,0:T(8,128)(2,1)}), bf16[9,512,512]{2,1,0:T(8,128)(2,1)}) %all-gather.3.cloned.1.call-update) | async-done | bytes 4718608 | tf_op jit(solution)/shard_map/all_gather | solution.py:364
  66.8 0.8 broadcast_in_dim.26.mask_ref
  67.6 6.9 %shard_map.238 = (f32[480,512]{1,0:T(8,128)}, f32[32,4,512]{2,1,0:T(4,128)}) custom-call(bf16[480,512]{1,0:T(8,128)(2,1)} %fusion.11.x_ref, f32[480,128]{1,0:T(8,128)} %broadcast_in_dim.26.mask_ref, bf16[9,512,512]{2,1,0:T(8,128)(2,1)} %all-gather.3.cloned.1.call-done.weight_hbm), custom_call_target="tpu_custom_call" | custom-call | tf_op jit(solution)/shard_map/pallas_call | solution.py:307
  74.6 3.1 all-to-all-start
  77.7 0.5 broadcast.102
  78.2 0.7 reduce
  78.9 0.1 reshape.117
  79.0 0.7 reshape.104.param_ref
  79.7 46.3 %all-gather.5.cloned.1.call-done.weight_hbm = bf16[9,512,512]{2,1,0:T(8,128)(2,1)} async-done(((bf16[9,32,512]{2,1,0:T(8,128)(2,1)}), bf16[9,512,512]{2,1,0:T(8,128)(2,1)}) %all-gather.5.cloned.1.call-update) | async-done | bytes 4718608 | tf_op jit(solution)/shard_map/all_gather | solution.py:365
  126.0 0.7 copy-done.2
  126.7 7.2 %shard_map.239 = (bf16[480,512]{1,0:T(8,128)(2,1)}, f32[480,512]{1,0:T(8,128)}, f32[4,512]{1,0:T(4,128)}, f32[32,4,512]{2,1,0:T(4,128)}) custom-call(f32[480,512]{1,0:T(8,128)} %get-tuple-element.30.hidden_ref, f32[32,4,512]{2,1,0:T(4,128)} %copy-done.2, f32[4,512]{1,0:T(4,128)} %reshape.104.param_ref, f32[480,128]{1,0:T(8,128)} %broadcast_in_dim.26.mask_ref, ...), custom_call_target="tpu_custom_call" | custom-call | tf_op jit(solution)/shard_map/pallas_call | solution.py:307
  134.0 3.2 all-to-all-start.2
  137.2 0.1 pad.66
  137.3 0.1 reshape.107
  137.5 0.1 reshape.105
  137.6 0.1 pad.65
  137.7 0.1 reshape.106
  137.7 0.8 fusion.13.back_ref
  138.6 8.9 %all-to-all-done.2.gathered_ref = f32[32,4,512]{2,1,0:T(4,128)S(1)} async-done(((f32[32,4,512]{2,1,0:T(4,128)}), f32[32,4,512]{2,1,0:T(4,128)S(1)}, u32[]{:S(2)}, u32[]{:S(2)}) %all-to-all-start.2) | async-done | bytes 262176 | tf_op jit(solution)/shard_map/all_to_all | solution.py:327
  147.4 0.7 copy-done.3
  148.1 3.6 shard_map.240
  151.8 11.5 %all_to_all.25.gathered_ref = f32[32,2,512]{2,1,0:T(2,128)} all-to-all(f32[32,2,512]{2,1,0:T(2,128)} %get-tuple-element.37), channel_id=1, replica_groups=mesh['dp'=2,'fsdp'=16] {'dp','fsdp'}, dimensions={0} | all-to-all | bytes 262144 | tf_op jit(solution)/shard_map/all_to_all | solution.py:327
  163.3 6.8 %shard_map.241 = (bf16[480,512]{1,0:T(8,128)(2,1)}, bf16[16,9,32,512]{3,2,1,0:T(8,128)(2,1)}, f32[2,512]{1,0:T(2,128)}) custom-call(f32[480,512]{1,0:T(8,128)} %get-tuple-element.35.grad_ref.residual_ref, f32[480,512]{1,0:T(8,128)} %get-tuple-element.32.second_ref, f32[4,512]{1,0:T(4,128)} %get-tuple-element.36.norm_ref, ...), custom_call_target="tpu_custom_call" | custom-call | tf_op jit(solution)/shard_map/pallas_call | solution.py:307
  170.2 7.4 %shard_map.242 = (f32[480,512]{1,0:T(8,128)}, f32[32,2,512]{2,1,0:T(2,128)}) custom-call(bf16[480,512]{1,0:T(8,128)(2,1)} %get-tuple-element.39.inner_ref, f32[480,512]{1,0:T(8,128)} %get-tuple-element.30.hidden_ref, f32[4,512]{1,0:T(4,128)} %get-tuple-element.40.norm_ref, f32[4,512]{1,0:T(4,128)} %reshape.104.param_ref, ...), custom_call_target="tpu_custom_call" | custom-call | tf_op jit(solution)/shard_map/pallas_call | solution.py:307
  177.5 11.5 %all_to_all.26.gathered_ref = f32[32,2,512]{2,1,0:T(2,128)} all-to-all(f32[32,2,512]{2,1,0:T(2,128)} %get-tuple-element.42), channel_id=1, replica_groups=mesh['dp'=2,'fsdp'=16] {'dp','fsdp'}, dimensions={0} | all-to-all | bytes 262144 | tf_op jit(solution)/shard_map/all_to_all | solution.py:327
  189.1 6.9 %shard_map.243 = (bf16[480,512]{1,0:T(8,128)(2,1)}, bf16[16,9,32,512]{3,2,1,0:T(8,128)(2,1)}, f32[2,512]{1,0:T(2,128)}) custom-call(f32[480,512]{1,0:T(8,128)} %get-tuple-element.41.grad_ref, f32[480,512]{1,0:T(8,128)} %get-tuple-element.30.hidden_ref, f32[4,512]{1,0:T(4,128)} %get-tuple-element.40.norm_ref, f32[32,2,512]{2,1,0:T(2,128)} %all_to_all.26.gathered_ref, ...), custom_call_target="tpu_custom_call" | custom-call | tf_op jit(solution)/shard_map/pallas_call | solution.py:307
  196.0 0.3 all-reduce.18.cloned.1.call-start
  196.3 0.7 copy-done.4
  197.1 0.1 reshape.108
  197.2 0.1 reshape.109
  197.2 0.1 reshape.110
  197.3 0.7 slice_bitcast_fusion.5
  198.0 0.8 slice_bitcast_fusion.4
  198.8 0.7 slice_bitcast_fusion.2
  199.5 6.9 %shard_map.244 = f32[480,512]{1,0:T(8,128)} custom-call(bf16[480,512]{1,0:T(8,128)(2,1)} %get-tuple-element.43.inner_ref, f32[480,512]{1,0:T(8,128)} %get-tuple-element.35.grad_ref.residual_ref, f32[480,128]{1,0:T(8,128)} %broadcast_in_dim.26.mask_ref, bf16[9,512,512]{2,1,0:T(8,128)(2,1)} %all-gather.3.cloned.1.call-done.weight_hbm), custom_call_target="tpu_custom_call" | custom-call | tf_op jit(solution)/shard_map/pallas_call | solution.py:307
  206.4 1.0 slice.65
  207.5 0.1 reshape.112
  207.7 0.7 slice_bitcast_fusion.3
  208.4 34.6 %reduce-scatter.5.cloned.1.call-done = bf16[1,9,32,512]{3,2,1,0:T(8,128)(2,1)} async-done(((bf16[16,9,32,512]{3,2,1,0:T(8,128)(2,1)}), bf16[1,9,32,512]{3,2,1,0:T(8,128)(2,1)}) %reduce-scatter.5.cloned.1.call-update) | async-done | bytes 294928 | tf_op jit(solution)/shard_map/reduce_scatter | solution.py:440
  243.0 78.8 %reduce-scatter.3.cloned.1.call-done = bf16[1,9,32,512]{3,2,1,0:T(8,128)(2,1)} async-done(((bf16[16,9,32,512]{3,2,1,0:T(8,128)(2,1)}), bf16[1,9,32,512]{3,2,1,0:T(8,128)(2,1)}) %reduce-scatter.3.cloned.1.call-update) | async-done | bytes 294928 | tf_op jit(solution)/shard_map/reduce_scatter | solution.py:440
  321.9 0.7 multiply_subtract_fusion
  322.6 0.2 reshape.113
  322.9 0.7 slice_bitcast_fusion.1
  323.6 0.8 slice_bitcast_fusion
  324.4 29.0 %all-reduce.18.cloned.1.call-done = (bf16[1,3,3,32,512]{4,3,2,1,0:T(8,128)(2,1)}, bf16[1,3,3,32,512]{4,3,2,1,0:T(8,128)(2,1)}) async-done(((bf16[1,3,3,32,512]{4,3,2,1,0:T(8,128)(2,1)}, bf16[1,3,3,32,512]{4,3,2,1,0:T(8,128)(2,1)}), (bf16[1,3,3,32,512]{4,3,2,1,0:T(8,128)(2,1)}, bf16[1,3,3,32,512]{4,3,2,1,0:T(8,128)(2,1)})) %all-reduce.18.cloned.1.call-update) | async-done | bytes 589840 | tf_op jit(solution)/shard_map/psum | solution.py:441
  353.4 4.5 %fusion.9 = (f32[2,3,3,512,32]{3,4,2,1,0:T(8,128)}, f32[2,3,3,512,32]{3,4,2,1,0:T(8,128)}, f32[2,3,3,512,32]{3,4,2,1,0:T(8,128)}) fusion(f32[2,3,3,512,32]{3,4,2,1,0:T(8,128)} %param.27, bf16[1,3,3,32,512]{4,3,2,1,0:T(8,128)(2,1)} %get-tuple-element.48, bf16[1,3,3,32,512]{4,3,2,1,0:T(8,128)(2,1)} %get-tuple-element.49, f32[2,3,3,512,32]{3,4,2,1,0:T(8,128)} %param.26, ...), kind=kLoop, calls=%fused_computation.16 | loop fusion | flops 4718592 | bytes 7667712 | tf_op jit(solution)/shard_map/transpose | solution.py:453
  (60 shorter events, 0.6 us)
Async XLA Ops:
  7.2 59.6 %all-gather.3.cloned.1.call-start = ((), (), s32[]{:S(2)}) async-start(), calls=%async_computation.7 | async-start | bytes 5013504 | tf_op jit(solution)/shard_map/all_gather | solution.py:364
  8.6 1.7 copy-start.13
  8.6 9.8 %copy-start.7 = (bf16[2,9,9,512]{3,0,2,1:T(2,128)(2,1)S(1)}, bf16[2,9,9,512]{3,0,2,1:T(2,128)(2,1)}, u32[]{:S(2)}) copy-start(bf16[2,9,9,512]{3,0,2,1:T(2,128)(2,1)} %param.17) | copy-start | bytes 497668
  8.6 10.0 %copy-start.5 = (bf16[6,5,5,512]{3,0,2,1:T(8,128)(2,1)S(1)}, bf16[6,5,5,512]{3,0,2,1:T(8,128)(2,1)}, u32[]{:S(2)}) copy-start(bf16[6,5,5,512]{3,0,2,1:T(8,128)(2,1)} %param.15) | copy-start | bytes 460804
  9.5 9.3 %copy-start.9 = (bf16[2,7,7,512]{3,0,2,1:T(2,128)(2,1)S(1)}, bf16[2,7,7,512]{3,0,2,1:T(2,128)(2,1)}, u32[]{:S(2)}) copy-start(bf16[2,7,7,512]{3,0,2,1:T(2,128)(2,1)} %param.16) | copy-start | bytes 301060
  9.5 116.5 %all-gather.5.cloned.1.call-start = ((), (), s32[]{:S(2)}) async-start(), calls=%async_computation.8 | async-start | bytes 5013504 | tf_op jit(solution)/shard_map/all_gather | solution.py:365
  9.6 9.3 %copy-start.12 = (s32[2,9,9]{2,0,1:T(2,128)S(1)}, s32[2,9,9]{2,0,1:T(2,128)}, u32[]{:S(2)}) copy-start(s32[2,9,9]{2,0,1:T(2,128)} %param.20) | copy-start | bytes 1948
  11.0 63.6 %all-to-all-start.1 = ((f32[16,1,128]{2,1,0:T(1,128)}), f32[16,1,128]{2,1,0:T(1,128)S(1)}, u32[]{:S(2)}, u32[]{:S(2)}) async-start(f32[16,1,128]{2,1,0:T(1,128)} %reshape.116), calls=%async_computation.1 | async-start | bytes 16384 | tf_op jit(solution)/shard_map/all_to_all | solution.py:369
  18.4 0.9 copy-start.11
  18.4 1.1 copy-start.14
  74.6 51.4 %all-to-all-start = ((f32[32,4,512]{2,1,0:T(4,128)}), f32[32,4,512]{2,1,0:T(4,128)S(1)}, u32[]{:S(2)}, u32[]{:S(2)}) async-start(f32[32,4,512]{2,1,0:T(4,128)} %get-tuple-element.31), calls=%async_computation | async-start | bytes 524288 | tf_op jit(solution)/shard_map/all_to_all | solution.py:327
  126.0 0.7 copy-start.2
  126.7 10.5 %copy-start.8 = (bf16[2,9,9,512]{3,0,2,1:T(2,128)(2,1)S(1)}, bf16[2,9,9,512]{3,0,2,1:T(2,128)(2,1)}, u32[]{:S(2)}) copy-start(bf16[2,9,9,512]{3,0,2,1:T(2,128)(2,1)} %param.23) | copy-start | bytes 497668
  133.9 3.5 copy-start.6
  134.0 3.6 copy-start.10
  134.0 13.5 %all-to-all-start.2 = ((f32[32,4,512]{2,1,0:T(4,128)}), f32[32,4,512]{2,1,0:T(4,128)S(1)}, u32[]{:S(2)}, u32[]{:S(2)}) async-start(f32[32,4,512]{2,1,0:T(4,128)} %get-tuple-element.33), calls=%async_computation.2 | async-start | bytes 524288 | tf_op jit(solution)/shard_map/all_to_all | solution.py:327
  137.1 105.9 %reduce-scatter.5.cloned.1.call-start = ((), (), s32[]{:S(2)}) async-start(), calls=%async_computation.10 | async-start | bytes 5013504 | tf_op jit(solution)/shard_map/reduce_scatter | solution.py:440
  147.4 0.7 copy-start.3
  170.1 151.7 %reduce-scatter.3.cloned.1.call-start = ((), (), s32[]{:S(2)}) async-start(), calls=%async_computation.9 | async-start | bytes 5013504 | tf_op jit(solution)/shard_map/reduce_scatter | solution.py:440
  196.0 1.0 copy-start.4
  196.0 157.3 %all-reduce.18.cloned.1.call-start = ((), (), s32[]{:S(2)}) async-start(), calls=%async_computation.11 | async-start | bytes 1179648 | tf_op jit(solution)/shard_map/psum | solution.py:441
  206.4 1.9 copy-start.1
  207.6 114.2 %copy-start.15 = (f32[2,512]{1,0:T(2,128)S(1)}, f32[2,512]{1,0:T(2,128)}, u32[]{:S(2)}) copy-start(f32[2,512]{1,0:T(2,128)} %get-tuple-element.47) | copy-start | bytes 12292
  207.6 114.2 %copy-start.16 = (f32[2,512]{1,0:T(2,128)S(1)}, f32[2,512]{1,0:T(2,128)}, u32[]{:S(2)}) copy-start(f32[2,512]{1,0:T(2,128)} %get-tuple-element.46) | copy-start | bytes 12292
  207.7 114.2 %copy-start.17 = (f32[4,32]{1,0:T(4,128)S(1)}, f32[4,32]{1,0:T(4,128)}, u32[]{:S(2)}) copy-start(f32[4,32]{1,0:T(4,128)} %param.28) | copy-start | bytes 1540
  207.7 114.2 %copy-start.18 = (f32[4,32]{1,0:T(4,128)S(1)}, f32[4,32]{1,0:T(4,128)}, u32[]{:S(2)}) copy-start(f32[4,32]{1,0:T(4,128)} %param.29) | copy-start | bytes 1540
  322.6 30.7 %copy-start = (f32[2,3,3,512,32]{3,4,2,1,0:T(8,128)S(1)}, f32[2,3,3,512,32]{3,4,2,1,0:T(8,128)}, u32[]{:S(2)}) copy-start(f32[2,3,3,512,32]{3,4,2,1,0:T(8,128)} %param.24) | copy-start | bytes 3538948
Sparse Core Ops, SparseCore 0:
  10.8 55.9 all-gather.2
  69.6 56.4 all-gather.4
  170.2 72.6 reduce-scatter.4
  247.2 74.5 reduce-scatter.2
  324.1 29.2 all-reduce.17

commit v2 on v1

v2 whole, which is shorter than its diff:
```python
import functools

import jax
import jax.numpy as jnp
from jax import lax
from jax.experimental import pallas as pl
from jax.experimental.pallas import tpu as pltpu
from jax.sharding import Mesh, PartitionSpec as P

STEP = 5
NORM_EPS = 1e-05
BETA_ONE = 0.5
BETA_TWO = 0.5
KERNEL_RATE = 0.03
NORM_RATE = 0.4
KERNEL_DECAY = 0.01
ADAM_EPS = 1e-08
TAPS = 9
LANES = 128
CELL = 2
VMEM_BYTES = 56 * 1024 * 1024
F32, BF16 = jnp.float32, jnp.bfloat16


def round_up(value, step):
    return (value + step - 1) // step * step


class Canvas:
    def __init__(self, shapes):
        self.shapes = shapes
        cells = [
            (side, group, first)
            for group, (count, side) in enumerate(shapes)
            for first in range(0, count, CELL)
        ]
        limit = max(
            sum(side + 1 for side, group, _ in cells if group == wanted)
            for wanted in range(len(shapes))
        )
        self.bands = []
        for side, group, first in sorted(cells, reverse=True):
            used = sum(cell[0] + 1 for cell in self.bands[-1]) if self.bands else limit
            if used + side + 1 > limit:
                self.bands.append([])
            self.bands[-1].append((side, group, first))
        self.width = limit
        self.right = CELL
        self.down = limit * CELL
        self.heights = [band[0][0] for band in self.bands]
        used_rows = (sum(self.heights) + len(self.bands) - 1) * self.down
        self.rows = round_up(used_rows, 16)
        self.halo = round_up(self.down + self.right, 8)
        self.lanes = round_up(self.rows + self.down + self.right, LANES)
        self.padded_rows = self.rows + 2 * self.halo

    def flatten(self, arrays):
        bands = []
        for band, height in zip(self.bands, self.heights):
            pieces = []
            for side, group, first in band:
                piece = jnp.transpose(arrays[group][first : first + CELL], (1, 2, 0, 3))
                piece = jnp.pad(piece, ((0, height + 1 - side), (0, 1), (0, 0), (0, 0)))
                pieces.append(piece)
            pieces = jnp.concatenate(pieces, axis=1)
            pieces = jnp.pad(pieces, ((0, 0), (0, self.width - pieces.shape[1]), (0, 0), (0, 0)))
            bands.append(pieces.reshape(-1, pieces.shape[3]))
        flat = jnp.concatenate(bands, axis=0)[: self.rows]
        return jnp.pad(flat, ((0, self.rows - flat.shape[0]), (0, 0)))

    def unflatten(self, flat):
        parts = [[] for _ in self.shapes]
        start = 0
        for band, height in zip(self.bands, self.heights):
            rows = flat[start : start + height * self.down]
            rows = rows.reshape(height, self.width, CELL, flat.shape[1])
            column = 0
            for side, group, first in band:
                piece = rows[:side, column : column + side]
                parts[group].append((first, jnp.transpose(piece, (2, 0, 1, 3))))
                column += side + 1
            start += (height + 1) * self.down
        return [
            jnp.concatenate([piece for _, piece in sorted(part, key=lambda item: item[0])], axis=0)
            for part in parts
        ]

    def shift(self, tap):
        return (tap // 3 - 1) * self.down + (tap % 3 - 1) * self.right

    def place(self, buffer, value):
        edge = jnp.zeros((self.halo, value.shape[1]), F32)
        buffer[0 : self.halo, :] = edge
        buffer[self.halo : self.halo + self.rows, :] = value
        buffer[self.halo + self.rows :, :] = edge

    def shifted(self, buffer, tap, sign):
        start = self.halo + sign * self.shift(tap)
        return buffer[start : start + self.rows, :].astype(BF16)


def wide(mask_ref, channels):
    return jnp.concatenate([mask_ref[...]] * (channels // LANES), axis=1)


def multiply(left, right, left_dim, right_dim):
    return lax.dot_general(
        left, right, (((left_dim,), (right_dim,)), ((), ())), preferred_element_type=F32
    )


def column_sum(value):
    return jnp.sum(value, axis=0, keepdims=True)


def spread_rows(rows, ref):
    ref[...] = jnp.broadcast_to(jnp.concatenate(rows, axis=0)[None], ref.shape)


def local_statistics(hidden, valid, ref):
    count = column_sum(valid)
    total = column_sum(hidden * valid)
    centre = total / jnp.maximum(count, 1.0)
    squares = column_sum(jnp.square(hidden - centre) * valid)
    spread_rows([total, squares, count, centre], ref)


def global_statistics(gathered):
    totals, squares, counts, centres = (gathered[:, row, :] for row in range(4))
    total = column_sum(counts)
    centre = column_sum(totals) / total
    between = column_sum(counts * jnp.square(centres - centre))
    spread = (column_sum(squares) + between) / total
    return centre, lax.rsqrt(spread + NORM_EPS), total


def sigmoid(value):
    return 1.0 / (1.0 + jnp.exp(-value))


def swish_slope(value):
    logistic = sigmoid(value)
    return logistic * (1.0 + value * (1.0 - logistic))


class Whole:
    def __init__(self, array):
        self.arrays = [array]

    @staticmethod
    def start(refs, weight, sem):
        copies = [pltpu.make_async_copy(refs[0], weight, sem)]
        copies[0].start()
        return copies


class Pieces:
    def __init__(self, pieces):
        self.arrays = [array for array, _ in pieces]
        self.slots = [slots for _, slots in pieces]

    def start(self, refs, weight, sem):
        y, z, x, c = (lax.axis_index(name) for name in ("y", "z", "x", "c"))
        copies = []
        for ref, slots in zip(refs, self.slots):
            _, _, width, half = ref.shape
            for slot, (dy, dz, dx, dc) in enumerate(slots):
                shard = ((z ^ dz) * 2 + (x ^ dx)) * 2 + (c ^ dc)
                row = pl.multiple_of(shard * width, width)
                lane = pl.multiple_of((y ^ dy) * half, half)
                copies.append(
                    pltpu.make_async_copy(
                        ref.at[slot], weight.at[:, pl.ds(row, width), pl.ds(lane, half)], sem
                    )
                )
        for copy in copies:
            copy.start()
        return copies


def convolve(canvas, value, source, refs, buffer, weight, sem, out_ref, sign, prepare=None):
    copies = source.start(refs, weight, sem)
    canvas.place(buffer, value() if callable(value) else value)
    for copy in copies:
        copy.wait()
    for tap in range(TAPS):
        part = canvas.shifted(buffer, tap, sign)
        product = multiply(part, weight[tap], 1, 1 if sign > 0 else 0)
        out_ref[...] = product if tap == 0 else out_ref[...] + product


def forward_one(canvas, source, x_ref, mask_ref, *refs):
    *weights, hidden_ref, stats_ref, buffer, weight, sem = refs
    convolve(
        canvas, lambda: x_ref[...].astype(F32), source, weights, buffer, weight, sem, hidden_ref, 1
    )
    local_statistics(hidden_ref[...], wide(mask_ref, x_ref.shape[1]), stats_ref)


def forward_two(canvas, source, hidden_ref, gathered_ref, param_ref, mask_ref, *refs):
    *weights, active_ref, second_ref, norm_ref, stats_ref, buffer, weight, sem = refs
    valid = wide(mask_ref, hidden_ref.shape[1])

    def active():
        centre, inv, total = global_statistics(gathered_ref)
        norm_ref[...] = jnp.concatenate([centre, inv, total, total], axis=0)
        value = (hidden_ref[...] - centre) * inv * param_ref[0:1, :] + param_ref[1:2, :]
        value = value * sigmoid(value) * valid
        active_ref[...] = value.astype(BF16)
        return value

    convolve(canvas, active, source, weights, buffer, weight, sem, second_ref, 1)
    local_statistics(second_ref[...], valid, stats_ref)


def turn(
    second_ref,
    gathered_ref,
    param_ref,
    mask_ref,
    x_ref,
    back_ref,
    result_ref,
    grad_ref,
    norm_ref,
    stats_ref,
):
    valid = wide(mask_ref, second_ref.shape[1])
    centre, inv, total = global_statistics(gathered_ref)
    norm_ref[...] = jnp.concatenate([centre, inv, total, total], axis=0)
    normed = (second_ref[...] - centre) * inv
    summed = normed * param_ref[2:3, :] + param_ref[3:4, :] + x_ref[...].astype(F32)
    logistic = sigmoid(summed)
    result_ref[...] = (summed * logistic * valid).astype(BF16)
    slope = logistic * (1.0 + summed * (1.0 - logistic))
    grad = back_ref[...].astype(F32) * valid * slope
    grad_ref[...] = grad
    spread_rows([column_sum(grad), column_sum(grad * normed)], stats_ref)


def norm_back(
    row,
    grad_ref,
    hidden_ref,
    norm_ref,
    gathered_ref,
    param_ref,
    mask_ref,
    inner_ref,
    sums_ref,
    turned_ref,
):
    valid = wide(mask_ref, grad_ref.shape[1])
    shift_grad = column_sum(gathered_ref[:, 0, :])
    gain_grad = column_sum(gathered_ref[:, 1, :])
    sums_ref[...] = jnp.concatenate([gain_grad, shift_grad], axis=0)
    centre, inv, total = norm_ref[0:1, :], norm_ref[1:2, :], norm_ref[2:3, :]
    normed = (hidden_ref[...] - centre) * inv
    grad = grad_ref[...] - shift_grad / total - normed * (gain_grad / total)
    inner = valid * (param_ref[row : row + 1, :] * inv) * grad
    inner_ref[...] = inner.astype(BF16)
    turned = jnp.transpose(inner).astype(BF16)
    rows, channels = inner.shape
    if len(turned_ref.shape) == 2:
        turned_ref[...] = turned
        return
    lanes = turned_ref.shape[-1]
    turned = jnp.concatenate([turned, jnp.zeros((channels, lanes - rows), BF16)], axis=1)
    half = channels // 32
    for shard in range(16):
        z, x, c = shard // 4, shard // 2 % 2, shard % 2
        for y in range(2):
            start = (shard * 2 + y) * half
            turned_ref[y, x, c, z * half : (z + 1) * half, :] = turned[start : start + half]


def backward_middle(canvas, source, inner_ref, hidden_ref, norm_ref, param_ref, mask_ref, *refs):
    *weights, grad_ref, stats_ref, buffer, weight, sem = refs
    valid = wide(mask_ref, hidden_ref.shape[1])
    convolve(
        canvas,
        lambda: inner_ref[...].astype(F32),
        source,
        weights,
        buffer,
        weight,
        sem,
        grad_ref,
        -1,
    )
    normed = (hidden_ref[...] - norm_ref[0:1, :]) * norm_ref[1:2, :]
    value = normed * param_ref[0:1, :] + param_ref[1:2, :]
    grad = grad_ref[...] * valid * swish_slope(value)
    grad_ref[...] = grad
    spread_rows([column_sum(grad), column_sum(grad * normed)], stats_ref)


def backward_input(canvas, source, inner_ref, residual_ref, mask_ref, *refs):
    *weights, grad_ref, buffer, weight, sem = refs
    convolve(
        canvas,
        lambda: inner_ref[...].astype(F32),
        source,
        weights,
        buffer,
        weight,
        sem,
        grad_ref,
        -1,
    )
    grad_ref[...] = residual_ref[...] + wide(mask_ref, grad_ref.shape[1]) * grad_ref[...]


def kernel_grad_whole(canvas, turned_ref, active_ref, out_ref, buffer):
    canvas.place(buffer, active_ref[...].astype(F32))
    for tap in range(TAPS):
        product = multiply(turned_ref[...], canvas.shifted(buffer, tap, 1), 1, 0)
        out_ref[tap] = product.astype(out_ref.dtype)


def kernel_grad_layer(canvas, turned_ref, *refs):
    *active_refs, send_ref, keep_ref, left, total = refs
    y, x, c = lax.axis_index("y"), lax.axis_index("x"), lax.axis_index("c")
    part = turned_ref.shape[3]
    for index, active_ref in enumerate(active_refs):
        block_y, block_x = y ^ (index // 2), x ^ (index % 2)
        for core in range(2):
            turned = turned_ref[block_y, block_x, c ^ core].astype(F32)
            for tap in range(TAPS):
                shift = canvas.shift(tap) % canvas.lanes
                moved = pltpu.roll(turned, shift, 1) if shift else turned
                row = (core * TAPS + tap) * part
                left[row : row + part, :] = moved[:, : canvas.rows].astype(BF16)
        product = multiply(left[...], active_ref[...], 1, 0)
        total[...] = product if index == 0 else total[...] + product
    half = part // 4
    for core, out_ref in enumerate((keep_ref, send_ref)):
        for tap in range(TAPS):
            for z in range(4):
                row = (core * TAPS + tap) * part + z * half
                out_ref[z, tap] = total[row : row + half, :].astype(out_ref.dtype)


def call(body, inputs, outputs, scratch=(), weights=()):
    whole = pl.BlockSpec(memory_space=pltpu.VMEM)
    return pl.pallas_call(
        body,
        out_shape=[jax.ShapeDtypeStruct(shape, dtype) for shape, dtype in outputs],
        in_specs=[whole] * len(inputs) + [pl.BlockSpec(memory_space=pl.ANY)] * len(weights),
        out_specs=[whole] * len(outputs),
        scratch_shapes=list(scratch),
        compiler_params=pltpu.CompilerParams(vmem_limit_bytes=VMEM_BYTES),
    )(*inputs, *weights)


def adamw(param, grad, first, second, rate, decay):
    first_new = BETA_ONE * first + (1.0 - BETA_ONE) * grad
    second_new = BETA_TWO * second + (1.0 - BETA_TWO) * grad * grad
    first_hat = first_new / (1.0 - BETA_ONE**STEP)
    second_hat = second_new / (1.0 - BETA_TWO**STEP)
    update = first_hat / (jnp.sqrt(second_hat) + ADAM_EPS)
    return (param - rate * (update + decay * param), first_new, second_new)


def flip(value, axis, bit, size):
    return lax.ppermute(value, axis, [(place, place ^ bit) for place in range(size)])


def diagonal(value):
    return lax.ppermute(value, ("y", "x"), [(place, place ^ 3) for place in range(4)])


class Grid:
    axes = ("y", "z", "x", "c")
    shard_axes = ("z", "x", "c")

    def weights(self, low):
        half = low.shape[2] // 2
        start = lax.axis_index("y") * half
        own = lax.dynamic_slice_in_dim(low, start, half, 2)[None]
        line = jnp.concatenate([own, flip(own, "z", 2, 4)], axis=0)
        line = jnp.concatenate([line, flip(line, "z", 1, 4)], axis=0)
        deep = (0, 2, 1, 3)
        over_x, over_y = flip(line, "x", 1, 2), flip(line, "y", 1, 2)
        last_x = flip(over_y[:2], "x", 1, 2)
        last_y = flip(over_x[2:], "y", 1, 2)
        pieces = [
            (line, [(0, dz, 0) for dz in deep]),
            (over_x, [(0, dz, 1) for dz in deep]),
            (over_y, [(1, dz, 0) for dz in deep]),
            (last_x, [(1, dz, 1) for dz in deep[:2]]),
            (last_y, [(1, dz, 1) for dz in deep[2:]]),
        ]
        found = []
        for array, slots in pieces:
            found.append((array, [slot + (0,) for slot in slots]))
            found.append((flip(array, "c", 1, 2), [slot + (1,) for slot in slots]))
        return Pieces(found)

    def layer(self, value):
        return [value, flip(value, "x", 1, 2), flip(value, "y", 1, 2), diagonal(value)]

    def turned_shape(self, canvas, channels):
        return ((2, 2, 2, channels // 8, canvas.lanes), BF16)

    def kernel_grad(self, canvas, turned, layer, channels):
        shape = turned.shape
        moved = lax.all_to_all(turned.reshape(4, *shape[2:]), ("y", "x"), 0, 0, tiled=True)
        half = channels // 32
        out = (4, TAPS, half, channels)
        send, keep = call(
            functools.partial(kernel_grad_layer, canvas),
            (moved.reshape(shape), *layer),
            ((out, BF16), (out, F32)),
            (
                pltpu.VMEM((2 * TAPS * shape[3], canvas.rows), BF16),
                pltpu.VMEM((2 * TAPS * shape[3], channels), F32),
            ),
        )
        chip = (keep + flip(send, "c", 1, 2).astype(F32)).astype(BF16)
        line = lax.all_to_all(chip, "z", 0, 0, tiled=True)
        own = jnp.sum(line.astype(F32), axis=0).astype(BF16)
        other = flip(own, "y", 1, 2)
        first = lax.axis_index("y") == 0
        halves = [jnp.where(first, own, other), jnp.where(first, other, own)]
        return jnp.concatenate(halves, axis=1).astype(F32)


class Plain:
    axes = ("dp", "fsdp")
    shard_axes = ("fsdp",)

    def weights(self, low):
        return Whole(lax.all_gather(low, "fsdp", axis=1, tiled=True))

    def layer(self, value):
        return [value]

    def turned_shape(self, canvas, channels):
        return ((channels, canvas.rows), BF16)

    def kernel_grad(self, canvas, turned, layer, channels):
        (full,) = call(
            functools.partial(kernel_grad_whole, canvas),
            (turned, layer[0]),
            (((TAPS, channels, channels), BF16),),
            (pltpu.VMEM((canvas.padded_rows, channels), F32),),
        )
        owned = lax.psum_scatter(full, "fsdp", scatter_dimension=1, tiled=True)
        return lax.psum(owned, "dp").astype(F32)


def local(
    ways,
    sizes,
    field_five,
    field_seven,
    field_nine,
    mask_five,
    mask_seven,
    mask_nine,
    back_five,
    back_seven,
    back_nine,
    kernels,
    norm_params,
    kernel_first,
    kernel_second,
    norm_first,
    norm_second,
):
    copies, shards = sizes
    fields = (field_five, field_seven, field_nine)
    masks = (mask_five, mask_seven, mask_nine)
    backs = (back_five, back_seven, back_nine)
    channels = field_five.shape[3]
    width = kernels.shape[4]
    canvas = Canvas([(field.shape[0], field.shape[1]) for field in fields])
    rows = canvas.rows
    count = copies * shards

    def turned(kernel):
        return jnp.transpose(kernel, (0, 1, 2, 4, 3)).reshape(2, TAPS, width, channels)

    def exchange(spread):
        return lax.all_to_all(spread, ways.axes, 0, 0, tiled=True)

    kernels_turned = turned(kernels)
    low = kernels_turned.astype(BF16)
    weight_one = ways.weights(low[0])
    weight_two = ways.weights(low[1])
    params = jnp.broadcast_to(norm_params.astype(BF16).astype(F32)[None], (shards, 4, width))
    params = lax.all_to_all(params, ways.shard_axes, 0, 0, tiled=True)
    params = jnp.transpose(params, (1, 0, 2)).reshape(4, channels)

    x = canvas.flatten([field * mask[..., None].astype(BF16) for field, mask in zip(fields, masks)])
    back = canvas.flatten(backs)
    mask = canvas.flatten([mask.astype(F32)[..., None] for mask in masks])
    mask = jnp.broadcast_to(mask, (rows, LANES))

    weighted = (
        pltpu.VMEM((canvas.padded_rows, channels), F32),
        pltpu.VMEM((TAPS, channels, channels), BF16),
        pltpu.SemaphoreType.DMA,
    )
    flat32 = ((rows, channels), F32)
    flat16 = ((rows, channels), BF16)
    four = ((count, 4, channels), F32)
    two = ((count, 2, channels), F32)
    norm = ((4, channels), F32)
    sums = ((2, channels), F32)
    turned_shape = ways.turned_shape(canvas, channels)

    def conv_call(body, source, inputs, outputs):
        return call(
            functools.partial(body, canvas, source), inputs, outputs, weighted, source.arrays
        )

    hidden, stats = conv_call(forward_one, weight_one, (x, mask), (flat32, four))
    gathered = exchange(stats)
    active, second, norm_one, stats = conv_call(
        forward_two, weight_two, (hidden, gathered, params, mask), (flat16, flat32, norm, four)
    )
    layer_active = ways.layer(active)
    layer_x = ways.layer(x)
    gathered = exchange(stats)
    result, grad_sum, norm_two, stats = call(
        turn, (second, gathered, params, mask, x, back), (flat16, flat32, norm, two)
    )
    gathered = exchange(stats)
    inner_two, sums_two, turned_two = call(
        functools.partial(norm_back, 2),
        (grad_sum, second, norm_two, gathered, params, mask),
        (flat16, sums, turned_shape),
    )
    grad_hidden, stats = conv_call(
        backward_middle, weight_two, (inner_two, hidden, norm_one, params, mask), (flat32, two)
    )
    gathered = exchange(stats)
    owned_two = ways.kernel_grad(canvas, turned_two, layer_active, channels)
    inner_one, sums_one, turned_one = call(
        functools.partial(norm_back, 0),
        (grad_hidden, hidden, norm_one, gathered, params, mask),
        (flat16, sums, turned_shape),
    )
    owned_one = ways.kernel_grad(canvas, turned_one, layer_x, channels)
    (grad_input,) = conv_call(backward_input, weight_one, (inner_one, grad_sum, mask), (flat32,))

    results = adamw(
        kernels_turned,
        jnp.stack([owned_one, owned_two]),
        turned(kernel_first),
        turned(kernel_second),
        KERNEL_RATE,
        KERNEL_DECAY,
    )
    kernel_results = [
        jnp.transpose(value.reshape(2, 3, 3, width, channels), (0, 1, 2, 4, 3))
        for value in results
    ]
    norm_full = jnp.concatenate([sums_one, sums_two], axis=0)
    place = lax.axis_index(ways.shard_axes) * width
    norm_grads = lax.dynamic_slice_in_dim(norm_full, place, width, 1)
    norm_results = adamw(norm_params, norm_grads, norm_first, norm_second, NORM_RATE, 0.0)
    return (
        *canvas.unflatten(result),
        *canvas.unflatten(grad_input),
        *kernel_results,
        *norm_results,
    )


def solution(mesh):
    sizes = (mesh.shape["dp"], mesh.shape["fsdp"])
    if sizes == (2, 16):
        ways = Grid()
        mesh = Mesh(mesh.devices.reshape(2, 4, 2, 2), ways.axes)
    else:
        ways = Plain()
    images = P(ways.axes, None, None, None)
    maps = P(ways.axes, None, None)
    weights = P(None, None, None, None, ways.shard_axes)
    norms = P(None, ways.shard_axes)
    in_specs = (
        (images,) * 3 + (maps,) * 3 + (images,) * 3 + (weights, norms, weights, weights, norms, norms)
    )
    out_specs = (images,) * 6 + (weights,) * 3 + (norms,) * 3
    body = functools.partial(local, ways, sizes)
    return jax.shard_map(body, mesh=mesh, in_specs=in_specs, out_specs=out_specs, check_vma=False)
```

time: 365 us -> 280 us (0.77)
  waiting for transfers between devices: 244 us -> 98.9 us
  starting transfers between devices: 14.1 us -> 60 us
  other arithmetic: 8.96 us -> 25.2 us
  local copies, waits for them, and re-layouts: 13.7 us -> 26.7 us
  between operations: 14.3 us -> 1.37 us
  blocking collectives: 23 us -> 11.5 us
  Pallas kernels: 45.9 us -> 54.8 us
    reduce_scatter x2 -> x0, waiting for transfers between devices: 113 us -> none  [reduced(): owned = lax.psum_scatter(value, 'fsdp', scatter_dimension=0, tiled=False)]
    all_gather x2 -> x0, waiting for transfers between devices: 92.4 us -> none  [the longest x1 46.3 us: local(): weight_two = lax.all_gather(low[1], 'fsdp', axis=1, tiled=True)]
    ppermute x0 -> x32, waiting for transfers between devices: none -> 69.1 us  [the longest x30 56.8 us: flip(): lax.ppermute(value, axis, [(place, place ^ bit) for place in range(size)])]
    ppermute x0 -> x32, starting transfers between devices: none -> 29.9 us  [the longest x30 27.7 us: flip(): lax.ppermute(value, axis, [(place, place ^ bit) for place in range(size)])]
    psum x1 -> x0, waiting for transfers between devices: 29 us -> none  [reduced(): return lax.psum(owned, 'dp').astype(f32)]
    all_to_all x3 -> x8, waiting for transfers between devices: 8.89 us -> 29.8 us  [the longest x2 14.4 us: kernel_grad(): line = lax.all_to_all(chip, 'z', 0, 0, tiled=True)]
    all_to_all x3 -> x8, starting transfers between devices: 13.7 us -> 30.1 us  [the longest x3 11.7 us: exchange(): return lax.all_to_all(spread, ways.axes, 0, 0, tiled=True)]
    all_to_all x2 -> x1, blocking collectives: 23 us -> 11.5 us  [exchange(): return lax.all_to_all(spread, ways.axes, 0, 0, tiled=True)]
  transfers between devices with their start and end apart: 8 -> 40, of which waited for: 6 -> 16; matrix products, arithmetic and copies ran while one was open for 4% -> 15% of each run, Pallas kernels for 8% -> 14%
where the time goes in v2:
time: 280 us; the launch traced here: 279 us
  waiting for transfers between devices  98.9 us (35%)
  starting transfers between devices  60 us (21%)
  Pallas kernels  54.8 us (20%)
  local copies, waits for them, and re-layouts  26.7 us (10%)
  other arithmetic  25.2 us (9%)
  blocking collectives  11.5 us (4%)
    ppermute x30, waiting for transfers between devices, flip(): lax.ppermute(value, axis, [(place, place ^ bit) for place in range(size)])  56.8 us
    pallas_call x9, Pallas kernels, call(): pl.pallas_call(body, out_shape=[jax.ShapeDtypeStruct(shape, dtype) for sh...  54.8 us
    ppermute x30, starting transfers between devices, flip(): lax.ppermute(value, axis, [(place, place ^ bit) for place in range(size)])  27.7 us
    all_to_all x2, waiting for transfers between devices, kernel_grad(): line = lax.all_to_all(chip, 'z', 0, 0, tiled=True)  14.4 us
    all_to_all x3, waiting for transfers between devices, exchange(): return lax.all_to_all(spread, ways.axes, 0, 0, tiled=True)  12.7 us
    ppermute x2, waiting for transfers between devices, diagonal(): lax.ppermute(value, ('y', 'x'), [(place, place ^ 3) for place in range(4)])  12.3 us
    all_to_all x3, starting transfers between devices, exchange(): return lax.all_to_all(spread, ways.axes, 0, 0, tiled=True)  11.7 us
    all_to_all x1, blocking collectives, exchange(): return lax.all_to_all(spread, ways.axes, 0, 0, tiled=True)  11.5 us
  transfers between devices with their start and end apart: 40, of which 16 were waited for; matrix products, arithmetic and copies ran while one was open for 15% of the time, Pallas kernels for 14%

profile of v2, /device:TPU:0, one launch (start us, length us, event | category | flops | bytes accessed | tf_op | source)
XLA Modules:
  0.0 278.6 jit_solution(4396386178549755324)
XLA Ops:
  0.6 1.4 bitcast_convert_fusion
  2.1 4.1 %collective-permute-start = (bf16[1,9,32,256]{3,2,1,0:T(8,128)(2,1)S(1)}, bf16[1,9,32,256]{3,2,1,0:T(8,128)(2,1)S(1)}, u32[]{:S(2)}, u32[]{:S(2)}) collective-permute-start(bf16[1,9,32,256]{3,2,1,0:T(8,128)(2,1)S(1)} %constant_dynamic-slice_fusion.1), channel_id=1, source_target_pairs={{0,8},{4,12},{8,0},{12,4},{1,9},{5,13},{9,1},{13,5},{2,10},{6,14},... | collective-permute-start | bytes 442376 | tf_op jit(solution)/shard_map/ppermute | solution.py:366
  7.0 4.0 %all-to-all-start.1 = ((f32[16,1,128]{2,1,0:T(1,128)}), f32[16,1,128]{2,1,0:T(1,128)}, u32[]{:S(2)}, u32[]{:S(2)}) async-start(f32[16,1,128]{2,1,0:T(1,128)} %reshape.180), calls=%async_computation.1 | async-start | bytes 16384 | tf_op jit(solution)/shard_map/all_to_all | solution.py:493
  11.0 2.8 %collective-permute-start.11 = (bf16[1,9,32,256]{3,2,1,0:T(8,128)(2,1)S(1)}, bf16[1,9,32,256]{3,2,1,0:T(8,128)(2,1)S(1)}, u32[]{:S(2)}, u32[]{:S(2)}) collective-permute-start(bf16[1,9,32,256]{3,2,1,0:T(8,128)(2,1)S(1)} %constant_dynamic-slice_fusion), channel_id=1, source_target_pairs={{0,8},{4,12},{8,0},{12,4},{1,9},{5,13},{9,1},{13,5},{2,10},{6,14},... | collective-permute-start | bytes 442376 | tf_op jit(solution)/shard_map/ppermute | solution.py:366
  16.8 1.5 collective-permute-start.1
  18.3 3.2 %collective-permute-done.11 = bf16[1,9,32,256]{3,2,1,0:T(8,128)(2,1)S(1)} collective-permute-done((bf16[1,9,32,256]{3,2,1,0:T(8,128)(2,1)S(1)}, bf16[1,9,32,256]{3,2,1,0:T(8,128)(2,1)S(1)}, u32[]{:S(2)}, u32[]{:S(2)}) %collective-permute-start.11) | collective-permute-done | bytes 147488 | tf_op jit(solution)/shard_map/ppermute | solution.py:366
  22.1 5.7 %collective-permute-done.1 = bf16[2,9,32,256]{3,2,1,0:T(8,128)(2,1)S(1)} collective-permute-done((bf16[2,9,32,256]{3,2,1,0:T(8,128)(2,1)S(1)}, bf16[2,9,32,256]{3,2,1,0:T(8,128)(2,1)S(1)}, u32[]{:S(2)}, u32[]{:S(2)}) %collective-permute-start.1) | collective-permute-done | bytes 294944 | tf_op jit(solution)/shard_map/ppermute | solution.py:366
  27.8 1.6 collective-permute-start.3
  29.5 1.5 collective-permute-start.5
  31.0 3.0 %collective-permute-done.12 = bf16[2,9,32,256]{3,2,1,0:T(8,128)(2,1)S(1)} collective-permute-done((bf16[2,9,32,256]{3,2,1,0:T(8,128)(2,1)S(1)}, bf16[2,9,32,256]{3,2,1,0:T(8,128)(2,1)S(1)}, u32[]{:S(2)}, u32[]{:S(2)}) %collective-permute-start.12) | collective-permute-done | bytes 294944 | tf_op jit(solution)/shard_map/ppermute | solution.py:366
  34.1 1.6 collective-permute-start.14
  35.7 1.5 collective-permute-start.16
  38.1 0.9 multiply_bitcast_fusion
  39.0 6.8 %collective-permute-done.5.refs_4_ = bf16[4,9,32,256]{3,2,1,0:T(8,128)(2,1)S(1)} collective-permute-done((bf16[4,9,32,256]{3,2,1,0:T(8,128)(2,1)S(1)}, bf16[4,9,32,256]{3,2,1,0:T(8,128)(2,1)S(1)}, u32[]{:S(2)}, u32[]{:S(2)}) %collective-permute-start.5) | collective-permute-done | bytes 589856 | tf_op jit(solution)/shard_map/ppermute | solution.py:366
  47.7 1.5 collective-permute-start.9
  50.1 1.7 reshape.165
  51.8 4.9 %collective-permute-done.14.refs_2_ = bf16[4,9,32,256]{3,2,1,0:T(8,128)(2,1)S(1)} collective-permute-done((bf16[4,9,32,256]{3,2,1,0:T(8,128)(2,1)S(1)}, bf16[4,9,32,256]{3,2,1,0:T(8,128)(2,1)S(1)}, u32[]{:S(2)}, u32[]{:S(2)}) %collective-permute-start.14) | collective-permute-done | bytes 589856 | tf_op jit(solution)/shard_map/ppermute | solution.py:366
  56.8 1.6 collective-permute-done.16.refs_4_
  58.4 2.2 fusion.14
  60.6 1.9 reshape.164
  62.5 2.0 pad_maximum_fusion.3.x_ref.refs_0_
  68.0 1.5 collective-permute-start.20
  71.0 1.4 copy.39
  72.4 1.0 reshape.167
  74.2 1.0 reshape.166
  76.2 7.4 %shard_map.238 = (f32[544,512]{1,0:T(8,128)}, f32[32,4,512]{2,1,0:T(4,128)}) custom-call(bf16[544,512]{1,0:T(8,128)(2,1)} %pad_maximum_fusion.3.x_ref.refs_0_, f32[544,128]{1,0:T(8,128)} %broadcast_in_dim.13.mask_ref, bf16[4,9,32,256]{3,2,1,0:T(8,128)(2,1)} %copy-done.2, bf16[4,9,32,256]{3,2,1,0:T(8,128)(2,1)} %collective-permute-done.2.refs_1_, ...), custom_call_target="tpu_custom_call" | custom-call | tf_op jit(solution)/shard_map/pallas_call | solution.py:346
  83.6 4.8 %all-to-all-start = ((f32[32,4,512]{2,1,0:T(4,128)}), f32[32,4,512]{2,1,0:T(4,128)}, u32[]{:S(2)}, u32[]{:S(2)}) async-start(f32[32,4,512]{2,1,0:T(4,128)} %get-tuple-element.35), calls=%async_computation | async-start | bytes 524288 | tf_op jit(solution)/shard_map/all_to_all | solution.py:486
  89.5 1.4 reduce.4
  91.6 1.4 copy.40
  93.0 1.4 reshape.168.param_ref
  94.5 4.2 %all-to-all-done.gathered_ref = f32[32,4,512]{2,1,0:T(4,128)} async-done(((f32[32,4,512]{2,1,0:T(4,128)}), f32[32,4,512]{2,1,0:T(4,128)}, u32[]{:S(2)}, u32[]{:S(2)}) %all-to-all-start) | async-done | bytes 262176 | tf_op jit(solution)/shard_map/all_to_all | solution.py:486
  98.7 8.0 %shard_map.239 = (bf16[544,512]{1,0:T(8,128)(2,1)}, f32[544,512]{1,0:T(8,128)}, f32[4,512]{1,0:T(4,128)}, f32[32,4,512]{2,1,0:T(4,128)}) custom-call(f32[544,512]{1,0:T(8,128)} %get-tuple-element.34.hidden_ref, f32[32,4,512]{2,1,0:T(4,128)} %all-to-all-done.gathered_ref, f32[4,512]{1,0:T(4,128)} %reshape.168.param_ref, ...), custom_call_target="tpu_custom_call" | custom-call | tf_op jit(solution)/shard_map/pallas_call | solution.py:346
  106.7 2.9 %all-to-all-start.2 = ((f32[32,4,512]{2,1,0:T(4,128)}), f32[32,4,512]{2,1,0:T(4,128)S(1)}, u32[]{:S(2)}, u32[]{:S(2)}) async-start(f32[32,4,512]{2,1,0:T(4,128)} %get-tuple-element.37), calls=%async_computation.2 | async-start | bytes 524288 | tf_op jit(solution)/shard_map/all_to_all | solution.py:486
  111.3 8.4 %all-to-all-done.2.gathered_ref = f32[32,4,512]{2,1,0:T(4,128)S(1)} async-done(((f32[32,4,512]{2,1,0:T(4,128)}), f32[32,4,512]{2,1,0:T(4,128)S(1)}, u32[]{:S(2)}, u32[]{:S(2)}) %all-to-all-start.2) | async-done | bytes 262176 | tf_op jit(solution)/shard_map/all_to_all | solution.py:486
  120.4 3.8 %shard_map.240 = (bf16[544,512]{1,0:T(8,128)(2,1)}, f32[544,512]{1,0:T(8,128)}, f32[4,512]{1,0:T(4,128)}, f32[32,2,512]{2,1,0:T(2,128)}) custom-call(f32[544,512]{1,0:T(8,128)} %get-tuple-element.36.second_ref.hidden_ref, f32[32,4,512]{2,1,0:T(4,128)} %copy-done.17, f32[4,512]{1,0:T(4,128)} %reshape.168.param_ref, f32[544,128]{1,0:T(8,128)} %broadcast_in_dim.13.mask_ref, ...), custom_call_target="tpu_custom_call" | custom-call | tf_op jit(solution)/shard_map/pallas_call | solution.py:346
  124.3 11.5 %all_to_all.45.gathered_ref = f32[32,2,512]{2,1,0:T(2,128)} all-to-all(f32[32,2,512]{2,1,0:T(2,128)} %get-tuple-element.41), channel_id=1, replica_groups=mesh['y'=2,'z'=4,'x'=2,'c'=2] {'y','z','x','c'}, dimensions={0} | all-to-all | bytes 262144 | tf_op jit(solution)/shard_map/all_to_all | solution.py:486
  135.8 3.1 %shard_map.241 = (bf16[544,512]{1,0:T(8,128)(2,1)}, f32[2,512]{1,0:T(2,128)}, bf16[2,2,2,64,640]{4,3,2,1,0:T(8,128)(2,1)}) custom-call(f32[544,512]{1,0:T(8,128)} %get-tuple-element.39.grad_ref.residual_ref, f32[544,512]{1,0:T(8,128)} %get-tuple-element.36.second_ref.hidden_ref, f32[4,512]{1,0:T(4,128)} %get-tuple-element.40.norm_ref, ...), custom_call_target="tpu_custom_call" | custom-call | tf_op jit(solution)/shard_map/pallas_call | solution.py:346
  138.8 3.6 %all-to-all-start.7 = ((bf16[4,2,64,640]{3,2,1,0:T(8,128)(2,1)}), bf16[4,2,64,640]{3,2,1,0:T(8,128)(2,1)S(1)}, u32[]{:S(2)}, u32[]{:S(2)}) async-start(bf16[4,2,64,640]{3,2,1,0:T(8,128)(2,1)} %bitcast.108), calls=%async_computation.7 | async-start | bytes 1310720 | tf_op jit(solution)/shard_map/all_to_all | solution.py:408
  142.5 2.0 collective-permute-start.27
  144.5 1.5 collective-permute-start.28
  146.0 8.2 %shard_map.242 = (f32[544,512]{1,0:T(8,128)}, f32[32,2,512]{2,1,0:T(2,128)}) custom-call(bf16[544,512]{1,0:T(8,128)(2,1)} %get-tuple-element.42.inner_ref, f32[544,512]{1,0:T(8,128)} %get-tuple-element.34.hidden_ref, f32[4,512]{1,0:T(4,128)} %get-tuple-element.43.norm_ref, f32[4,512]{1,0:T(4,128)} %reshape.168.param_ref, ...), custom_call_target="tpu_custom_call" | custom-call | tf_op jit(solution)/shard_map/pallas_call | solution.py:346
  154.2 4.0 %all-to-all-start.4 = ((f32[32,2,512]{2,1,0:T(2,128)}), f32[32,2,512]{2,1,0:T(2,128)}, u32[]{:S(2)}, u32[]{:S(2)}) async-start(f32[32,2,512]{2,1,0:T(2,128)} %get-tuple-element.45), calls=%async_computation.4 | async-start | bytes 262144 | tf_op jit(solution)/shard_map/all_to_all | solution.py:486
  158.2 8.0 %collective-permute-done.27.refs_1_ = bf16[544,512]{1,0:T(8,128)(2,1)S(1)} collective-permute-done((bf16[544,512]{1,0:T(8,128)(2,1)S(1)}, bf16[544,512]{1,0:T(8,128)(2,1)S(1)}, u32[]{:S(2)}, u32[]{:S(2)}) %collective-permute-start.27) | collective-permute-done | bytes 557088 | tf_op jit(solution)/shard_map/ppermute | solution.py:366
  166.2 12.3 %collective-permute-done.29.refs_3_ = bf16[544,512]{1,0:T(8,128)(2,1)S(1)} collective-permute-done((bf16[544,512]{1,0:T(8,128)(2,1)S(1)}, bf16[544,512]{1,0:T(8,128)(2,1)S(1)}, u32[]{:S(2)}, u32[]{:S(2)}) %collective-permute-start.29) | collective-permute-done | bytes 557088 | tf_op jit(solution)/shard_map/ppermute | solution.py:370
  179.4 6.8 %shard_map.246 = (bf16[4,9,16,512]{3,2,1,0:T(8,128)(2,1)}, f32[4,9,16,512]{3,2,1,0:T(8,128)}) custom-call(bf16[2,2,2,64,640]{4,3,2,1,0:T(8,128)(2,1)} %bitcast.104, bf16[544,512]{1,0:T(8,128)(2,1)} %get-tuple-element.51.refs_0_, bf16[544,512]{1,0:T(8,128)(2,1)} %copy-done.21, bf16[544,512]{1,0:T(8,128)(2,1)} %copy-done.22, bf16[544,512]{1,0:T(8,128)(2,1)} %copy-done.23), custom_call_target="tpu_custom_call" | custom-call | tf_op jit(solution)/shard_map/pallas_call | solution.py:346
  187.7 2.1 collective-permute-start.24
  189.8 3.1 %shard_map.243 = (bf16[544,512]{1,0:T(8,128)(2,1)}, f32[2,512]{1,0:T(2,128)}, bf16[2,2,2,64,640]{4,3,2,1,0:T(8,128)(2,1)}) custom-call(f32[544,512]{1,0:T(8,128)} %get-tuple-element.44.grad_ref, f32[544,512]{1,0:T(8,128)} %get-tuple-element.34.hidden_ref, f32[4,512]{1,0:T(4,128)} %get-tuple-element.43.norm_ref, f32[32,2,512]{2,1,0:T(2,128)} %all-to-all-done.4.gathered_ref, ...), custom_call_target="tpu_custom_call" | custom-call | tf_op jit(solution)/shard_map/pallas_call | solution.py:346
  192.9 3.7 %all-to-all-start.5 = ((bf16[4,2,64,640]{3,2,1,0:T(8,128)(2,1)}), bf16[4,2,64,640]{3,2,1,0:T(8,128)(2,1)S(1)}, u32[]{:S(2)}, u32[]{:S(2)}) async-start(bf16[4,2,64,640]{3,2,1,0:T(8,128)(2,1)} %bitcast.107), calls=%async_computation.5 | async-start | bytes 1310720 | tf_op jit(solution)/shard_map/all_to_all | solution.py:408
  196.6 0.9 slice.134
  197.7 4.1 %collective-permute-done.22.refs_1_ = bf16[544,512]{1,0:T(8,128)(2,1)S(1)} collective-permute-done((bf16[544,512]{1,0:T(8,128)(2,1)S(1)}, bf16[544,512]{1,0:T(8,128)(2,1)S(1)}, u32[]{:S(2)}, u32[]{:S(2)}) %collective-permute-start.22) | collective-permute-done | bytes 557088 | tf_op jit(solution)/shard_map/ppermute | solution.py:366
  201.8 16.1 %collective-permute-done.23.refs_2_ = bf16[544,512]{1,0:T(8,128)(2,1)S(1)} collective-permute-done((bf16[544,512]{1,0:T(8,128)(2,1)S(1)}, bf16[544,512]{1,0:T(8,128)(2,1)S(1)}, u32[]{:S(2)}, u32[]{:S(2)}) %collective-permute-start.23) | collective-permute-done | bytes 557088 | tf_op jit(solution)/shard_map/ppermute | solution.py:366
  217.9 2.7 all-to-all-done.5
  221.4 6.9 %shard_map.245 = (bf16[4,9,16,512]{3,2,1,0:T(8,128)(2,1)}, f32[4,9,16,512]{3,2,1,0:T(8,128)}) custom-call(bf16[2,2,2,64,640]{4,3,2,1,0:T(8,128)(2,1)} %bitcast.103, bf16[544,512]{1,0:T(8,128)(2,1)} %pad_maximum_fusion.3.x_ref.refs_0_, bf16[544,512]{1,0:T(8,128)(2,1)} %copy-done.19, bf16[544,512]{1,0:T(8,128)(2,1)} %copy-done.20, ...), custom_call_target="tpu_custom_call" | custom-call | tf_op jit(solution)/shard_map/pallas_call | solution.py:346
  228.3 1.1 add_convert_fusion
  229.4 3.6 %all-to-all-start.8 = ((bf16[4,9,16,512]{3,2,1,0:T(8,128)(2,1)}), bf16[4,9,16,512]{3,2,1,0:T(8,128)(2,1)S(1)}, u32[]{:S(2)}, u32[]{:S(2)}) async-start(bf16[4,9,16,512]{3,2,1,0:T(8,128)(2,1)} %add_convert_fusion), calls=%async_computation.8 | async-start | bytes 1179648 | tf_op jit(solution)/shard_map/all_to_all | solution.py:421
  235.7 7.6 %shard_map.244 = f32[544,512]{1,0:T(8,128)} custom-call(bf16[544,512]{1,0:T(8,128)(2,1)} %get-tuple-element.46.inner_ref, f32[544,512]{1,0:T(8,128)} %get-tuple-element.39.grad_ref.residual_ref, f32[544,128]{1,0:T(8,128)} %broadcast_in_dim.13.mask_ref, bf16[4,9,32,256]{3,2,1,0:T(8,128)(2,1)} %copy-done.2, ...), custom_call_target="tpu_custom_call" | custom-call | tf_op jit(solution)/shard_map/pallas_call | solution.py:346
  243.3 1.1 slice-done
  244.8 2.3 add_convert_fusion.1
  247.1 2.7 all-to-all-done.8
  249.8 3.5 %all-to-all-start.6 = ((bf16[4,9,16,512]{3,2,1,0:T(8,128)(2,1)}), bf16[4,9,16,512]{3,2,1,0:T(8,128)(2,1)S(1)}, u32[]{:S(2)}, u32[]{:S(2)}) async-start(bf16[4,9,16,512]{3,2,1,0:T(8,128)(2,1)} %add_convert_fusion.1), calls=%async_computation.6 | async-start | bytes 1179648 | tf_op jit(solution)/shard_map/all_to_all | solution.py:421
  257.6 11.7 %all-to-all-done.6 = bf16[4,9,16,512]{3,2,1,0:T(8,128)(2,1)S(1)} async-done(((bf16[4,9,16,512]{3,2,1,0:T(8,128)(2,1)}), bf16[4,9,16,512]{3,2,1,0:T(8,128)(2,1)S(1)}, u32[]{:S(2)}, u32[]{:S(2)}) %all-to-all-start.6) | async-done | bytes 589856 | tf_op jit(solution)/shard_map/all_to_all | solution.py:421
  270.2 0.9 broadcast_select_fusion.1
  271.2 3.4 %collective-permute-done.26 = bf16[9,16,512]{2,1,0:T(8,128)(2,1)S(1)} collective-permute-done((bf16[9,16,512]{2,1,0:T(8,128)(2,1)S(1)}, bf16[9,16,512]{2,1,0:T(8,128)(2,1)S(1)}, u32[]{:S(2)}, u32[]{:S(2)}) %collective-permute-start.26) | collective-permute-done | bytes 147488 | tf_op jit(solution)/shard_map/ppermute | solution.py:366
  274.6 3.9 %fusion.9 = (f32[2,3,3,512,32]{3,4,2,1,0:T(8,128)}, f32[2,3,3,512,32]{3,4,2,1,0:T(8,128)}, f32[2,3,3,512,32]{3,4,2,1,0:T(8,128)}) fusion(f32[2,3,3,512,32]{3,4,2,1,0:T(8,128)S(1)} %copy-done.14, bf16[1,3,3,16,512]{4,3,2,1,0:T(8,128)(2,1)S(1)} %bitcast.110, bf16[1,3,3,16,512]{4,3,2,1,0:T(8,128)(2,1)S(1)} %bitcast.109, ...), kind=kLoop, calls=%fused_computation.19 | loop fusion | flops 6488064 | bytes 7667712 | tf_op jit(solution)/shard_map/transpose | solution.py:558
  (186 shorter events, 30.7 us)
Async XLA Ops:
  2.0 11.7 %copy-start.33 = (s32[6,5,5]{2,0,1:T(8,128)S(1)}, s32[6,5,5]{2,0,1:T(8,128)}, u32[]{:S(2)}) copy-start(s32[6,5,5]{2,0,1:T(8,128)} %param.18) | copy-start | bytes 1804
  2.0 12.5 %copy-start.34 = (s32[2,9,9]{2,0,1:T(2,128)S(1)}, s32[2,9,9]{2,0,1:T(2,128)}, u32[]{:S(2)}) copy-start(s32[2,9,9]{2,0,1:T(2,128)} %param.20) | copy-start | bytes 1948
  2.0 13.1 %copy-start.25 = (bf16[6,5,5,512]{3,0,2,1:T(8,128)(2,1)S(1)}, bf16[6,5,5,512]{3,0,2,1:T(8,128)(2,1)}, u32[]{:S(2)}) copy-start(bf16[6,5,5,512]{3,0,2,1:T(8,128)(2,1)} %param.15) | copy-start | bytes 460804
  2.1 13.2 %copy-start.37 = (s32[2,7,7]{2,0,1:T(2,128)S(1)}, s32[2,7,7]{2,0,1:T(2,128)}, u32[]{:S(2)}) copy-start(s32[2,7,7]{2,0,1:T(2,128)} %param.19) | copy-start | bytes 1180
  2.1 14.6 %collective-permute-start = (bf16[1,9,32,256]{3,2,1,0:T(8,128)(2,1)S(1)}, bf16[1,9,32,256]{3,2,1,0:T(8,128)(2,1)S(1)}, u32[]{:S(2)}, u32[]{:S(2)}) collective-permute-start(bf16[1,9,32,256]{3,2,1,0:T(8,128)(2,1)S(1)} %constant_dynamic-slice_fusion.1), channel_id=1, source_target_pairs={{0,8},{4,12},{8,0},{12,4},{1,9},{5,13},{9,1},{13,5},{2,10},{6,14},... | collective-permute-start | bytes 442376 | tf_op jit(solution)/shard_map/ppermute | solution.py:366
  7.0 76.7 %all-to-all-start.1 = ((f32[16,1,128]{2,1,0:T(1,128)}), f32[16,1,128]{2,1,0:T(1,128)}, u32[]{:S(2)}, u32[]{:S(2)}) async-start(f32[16,1,128]{2,1,0:T(1,128)} %reshape.180), calls=%async_computation.1 | async-start | bytes 16384 | tf_op jit(solution)/shard_map/all_to_all | solution.py:493
  11.0 10.5 %collective-permute-start.11 = (bf16[1,9,32,256]{3,2,1,0:T(8,128)(2,1)S(1)}, bf16[1,9,32,256]{3,2,1,0:T(8,128)(2,1)S(1)}, u32[]{:S(2)}, u32[]{:S(2)}) collective-permute-start(bf16[1,9,32,256]{3,2,1,0:T(8,128)(2,1)S(1)} %constant_dynamic-slice_fusion), channel_id=1, source_target_pairs={{0,8},{4,12},{8,0},{12,4},{1,9},{5,13},{9,1},{13,5},{2,10},{6,14},... | collective-permute-start | bytes 442376 | tf_op jit(solution)/shard_map/ppermute | solution.py:366
  16.8 11.0 %collective-permute-start.1 = (bf16[2,9,32,256]{3,2,1,0:T(8,128)(2,1)S(1)}, bf16[2,9,32,256]{3,2,1,0:T(8,128)(2,1)S(1)}, u32[]{:S(2)}, u32[]{:S(2)}) collective-permute-start(bf16[2,9,32,256]{3,2,1,0:T(8,128)(2,1)S(1)} %pad_maximum_fusion.5), channel_id=1, source_target_pairs={{0,4},{4,0},{8,12},{12,8},{1,5},{5,1},{9,13},{13,9},{2,6},{6,2},{1... | collective-permute-start | bytes 884744 | tf_op jit(solution)/shard_map/ppermute | solution.py:366
  21.5 12.5 %collective-permute-start.12 = (bf16[2,9,32,256]{3,2,1,0:T(8,128)(2,1)S(1)}, bf16[2,9,32,256]{3,2,1,0:T(8,128)(2,1)S(1)}, u32[]{:S(2)}, u32[]{:S(2)}) collective-permute-start(bf16[2,9,32,256]{3,2,1,0:T(8,128)(2,1)S(1)} %pad_maximum_fusion.6), channel_id=1, source_target_pairs={{0,4},{4,0},{8,12},{12,8},{1,5},{5,1},{9,13},{13,9},{2,6},{6,2},{1... | collective-permute-start | bytes 884744 | tf_op jit(solution)/shard_map/ppermute | solution.py:366
  22.1 15.2 %copy-start.31 = (bf16[2,7,7,512]{3,0,2,1:T(2,128)(2,1)S(1)}, bf16[2,7,7,512]{3,0,2,1:T(2,128)(2,1)}, u32[]{:S(2)}) copy-start(bf16[2,7,7,512]{3,0,2,1:T(2,128)(2,1)} %param.16) | copy-start | bytes 301060
  22.1 16.0 %copy-start.26 = (bf16[2,9,9,512]{3,0,2,1:T(2,128)(2,1)S(1)}, bf16[2,9,9,512]{3,0,2,1:T(2,128)(2,1)}, u32[]{:S(2)}) copy-start(bf16[2,9,9,512]{3,0,2,1:T(2,128)(2,1)} %param.17) | copy-start | bytes 497668
  22.1 16.0 %copy-start.28 = (bf16[2,9,9]{0,2,1:T(8,128)(2,1)S(1)}, bf16[2,9,9]{0,2,1:T(8,128)(2,1)}, u32[]{:S(2)}) copy-start(bf16[2,9,9]{0,2,1:T(8,128)(2,1)} %copy.35) | copy-start | bytes 976
  27.8 24.0 %copy-start.2 = (bf16[4,9,32,256]{3,2,1,0:T(8,128)(2,1)}, bf16[4,9,32,256]{3,2,1,0:T(8,128)(2,1)S(1)}, u32[]{:S(2)}) copy-start(bf16[4,9,32,256]{3,2,1,0:T(8,128)(2,1)S(1)} %pad_maximum_fusion.refs_0_) | copy-start | bytes 1769476
  27.8 19.1 %collective-permute-start.3 = (bf16[4,9,32,256]{3,2,1,0:T(8,128)(2,1)S(1)}, bf16[4,9,32,256]{3,2,1,0:T(8,128)(2,1)S(1)}, u32[]{:S(2)}, u32[]{:S(2)}) collective-permute-start(bf16[4,9,32,256]{3,2,1,0:T(8,128)(2,1)S(1)} %pad_maximum_fusion.refs_0_), channel_id=1, source_target_pairs={{0,2},{2,0},{1,3},{3,1},{4,6},{6,4},{5,7},{7,5},{8,10},{10,8},{9,1... | collective-permute-start | bytes 1769480 | tf_op jit(solution)/shard_map/ppermute | solution.py:366
  29.5 16.2 %collective-permute-start.5 = (bf16[4,9,32,256]{3,2,1,0:T(8,128)(2,1)S(1)}, bf16[4,9,32,256]{3,2,1,0:T(8,128)(2,1)S(1)}, u32[]{:S(2)}, u32[]{:S(2)}) collective-permute-start(bf16[4,9,32,256]{3,2,1,0:T(8,128)(2,1)S(1)} %pad_maximum_fusion.refs_0_), channel_id=1, source_target_pairs={{0,16},{16,0},{1,17},{17,1},{2,18},{18,2},{3,19},{19,3},{4,20},{20... | collective-permute-start | bytes 1769480 | tf_op jit(solution)/shard_map/ppermute | solution.py:366
  34.1 33.2 %copy-start.1 = (bf16[4,9,32,256]{3,2,1,0:T(8,128)(2,1)}, bf16[4,9,32,256]{3,2,1,0:T(8,128)(2,1)S(1)}, u32[]{:S(2)}) copy-start(bf16[4,9,32,256]{3,2,1,0:T(8,128)(2,1)S(1)} %pad_maximum_fusion.1.refs_0_) | copy-start | bytes 1769476
  34.1 22.7 %collective-permute-start.14 = (bf16[4,9,32,256]{3,2,1,0:T(8,128)(2,1)S(1)}, bf16[4,9,32,256]{3,2,1,0:T(8,128)(2,1)S(1)}, u32[]{:S(2)}, u32[]{:S(2)}) collective-permute-start(bf16[4,9,32,256]{3,2,1,0:T(8,128)(2,1)S(1)} %pad_maximum_fusion.1.refs_0_), channel_id=1, source_target_pairs={{0,2},{2,0},{1,3},{3,1},{4,6},{6,4},{5,7},{7,5},{8,10},{10,8},{9,1... | collective-permute-start | bytes 1769480 | tf_op jit(solution)/shard_map/ppermute | solution.py:366
  35.7 22.7 %collective-permute-start.16 = (bf16[4,9,32,256]{3,2,1,0:T(8,128)(2,1)S(1)}, bf16[4,9,32,256]{3,2,1,0:T(8,128)(2,1)S(1)}, u32[]{:S(2)}, u32[]{:S(2)}) collective-permute-start(bf16[4,9,32,256]{3,2,1,0:T(8,128)(2,1)S(1)} %pad_maximum_fusion.1.refs_0_), channel_id=1, source_target_pairs={{0,16},{16,0},{1,17},{17,1},{2,18},{18,2},{3,19},{19,3},{4,20},{20... | collective-permute-start | bytes 1769480 | tf_op jit(solution)/shard_map/ppermute | solution.py:366
  45.7 14.8 %copy-start.7 = (bf16[4,9,32,256]{3,2,1,0:T(8,128)(2,1)}, bf16[4,9,32,256]{3,2,1,0:T(8,128)(2,1)S(1)}, u32[]{:S(2)}) copy-start(bf16[4,9,32,256]{3,2,1,0:T(8,128)(2,1)S(1)} %collective-permute-done.5.refs_4_) | copy-start | bytes 1769476
  46.5 17.9 %collective-permute-start.7 = (bf16[2,9,32,256]{3,2,1,0:T(8,128)(2,1)}, bf16[2,9,32,256]{3,2,1,0:T(8,128)(2,1)}, u32[]{:S(2)}, u32[]{:S(2)}) collective-permute-start(bf16[2,9,32,256]{3,2,1,0:T(8,128)(2,1)} %slice.155), channel_id=1, source_target_pairs={{0,2},{2,0},{1,3},{3,1},{4,6},{6,4},{5,7},{7,5},{8,10},{10,8},{9,1... | collective-permute-start | bytes 884744 | tf_op jit(solution)/shard_map/ppermute | solution.py:366
  47.0 15.5 %copy-start.6 = (bf16[4,9,32,256]{3,2,1,0:T(8,128)(2,1)}, bf16[4,9,32,256]{3,2,1,0:T(8,128)(2,1)S(1)}, u32[]{:S(2)}) copy-start(bf16[4,9,32,256]{3,2,1,0:T(8,128)(2,1)S(1)} %collective-permute-done.3.refs_2_) | copy-start | bytes 1769476
  47.7 17.0 %collective-permute-start.9 = (bf16[2,9,32,256]{3,2,1,0:T(8,128)(2,1)}, bf16[2,9,32,256]{3,2,1,0:T(8,128)(2,1)}, u32[]{:S(2)}, u32[]{:S(2)}) collective-permute-start(bf16[2,9,32,256]{3,2,1,0:T(8,128)(2,1)} %slice.156), channel_id=1, source_target_pairs={{0,16},{16,0},{1,17},{17,1},{2,18},{18,2},{3,19},{19,3},{4,20},{20... | collective-permute-start | bytes 884744 | tf_op jit(solution)/shard_map/ppermute | solution.py:366
  51.8 15.4 %collective-permute-start.2 = (bf16[4,9,32,256]{3,2,1,0:T(8,128)(2,1)S(1)}, bf16[4,9,32,256]{3,2,1,0:T(8,128)(2,1)}, u32[]{:S(2)}, u32[]{:S(2)}) collective-permute-start(bf16[4,9,32,256]{3,2,1,0:T(8,128)(2,1)S(1)} %pad_maximum_fusion.refs_0_), channel_id=1, source_target_pairs={{0,1},{1,0},{2,3},{3,2},{4,5},{5,4},{6,7},{7,6},{8,9},{9,8},{10,11... | collective-permute-start | bytes 1769480 | tf_op jit(solution)/shard_map/ppermute | solution.py:366
  56.8 12.7 %copy-start.4 = (bf16[4,9,32,256]{3,2,1,0:T(8,128)(2,1)}, bf16[4,9,32,256]{3,2,1,0:T(8,128)(2,1)S(1)}, u32[]{:S(2)}) copy-start(bf16[4,9,32,256]{3,2,1,0:T(8,128)(2,1)S(1)} %collective-permute-done.14.refs_2_) | copy-start | bytes 1769476
  56.8 10.8 %collective-permute-start.4 = (bf16[4,9,32,256]{3,2,1,0:T(8,128)(2,1)S(1)}, bf16[4,9,32,256]{3,2,1,0:T(8,128)(2,1)}, u32[]{:S(2)}, u32[]{:S(2)}) collective-permute-start(bf16[4,9,32,256]{3,2,1,0:T(8,128)(2,1)S(1)} %collective-permute-done.3.refs_2_), channel_id=1, source_target_pairs={{0,1},{1,0},{2,3},{3,2},{4,5},{5,4},{6,7},{7,6},{8,9},{9,8},{10,11... | collective-permute-start | bytes 1769480 | tf_op jit(solution)/shard_map/ppermute | solution.py:366
  58.4 11.2 %copy-start.5 = (bf16[4,9,32,256]{3,2,1,0:T(8,128)(2,1)}, bf16[4,9,32,256]{3,2,1,0:T(8,128)(2,1)S(1)}, u32[]{:S(2)}) copy-start(bf16[4,9,32,256]{3,2,1,0:T(8,128)(2,1)S(1)} %collective-permute-done.16.refs_4_) | copy-start | bytes 1769476
  58.4 9.6 %collective-permute-start.6 = (bf16[4,9,32,256]{3,2,1,0:T(8,128)(2,1)S(1)}, bf16[4,9,32,256]{3,2,1,0:T(8,128)(2,1)}, u32[]{:S(2)}, u32[]{:S(2)}) collective-permute-start(bf16[4,9,32,256]{3,2,1,0:T(8,128)(2,1)S(1)} %collective-permute-done.5.refs_4_), channel_id=1, source_target_pairs={{0,1},{1,0},{2,3},{3,2},{4,5},{5,4},{6,7},{7,6},{8,9},{9,8},{10,11... | collective-permute-start | bytes 1769480 | tf_op jit(solution)/shard_map/ppermute | solution.py:366
  64.4 5.1 %collective-permute-start.8 = (bf16[2,9,32,256]{3,2,1,0:T(8,128)(2,1)}, bf16[2,9,32,256]{3,2,1,0:T(8,128)(2,1)S(1)}, u32[]{:S(2)}, u32[]{:S(2)}) collective-permute-start(bf16[2,9,32,256]{3,2,1,0:T(8,128)(2,1)} %collective-permute-done.7.refs_6_), channel_id=1, source_target_pairs={{0,1},{1,0},{2,3},{3,2},{4,5},{5,4},{6,7},{7,6},{8,9},{9,8},{10,11... | collective-permute-start | bytes 884744 | tf_op jit(solution)/shard_map/ppermute | solution.py:366
  64.7 4.9 %collective-permute-start.10 = (bf16[2,9,32,256]{3,2,1,0:T(8,128)(2,1)}, bf16[2,9,32,256]{3,2,1,0:T(8,128)(2,1)S(1)}, u32[]{:S(2)}, u32[]{:S(2)}) collective-permute-start(bf16[2,9,32,256]{3,2,1,0:T(8,128)(2,1)} %collective-permute-done.9.refs_8_), channel_id=1, source_target_pairs={{0,1},{1,0},{2,3},{3,2},{4,5},{5,4},{6,7},{7,6},{8,9},{9,8},{10,11... | collective-permute-start | bytes 884744 | tf_op jit(solution)/shard_map/ppermute | solution.py:366
  67.2 27.2 %collective-permute-start.13 = (bf16[4,9,32,256]{3,2,1,0:T(8,128)(2,1)S(1)}, bf16[4,9,32,256]{3,2,1,0:T(8,128)(2,1)S(1)}, u32[]{:S(2)}, u32[]{:S(2)}) collective-permute-start(bf16[4,9,32,256]{3,2,1,0:T(8,128)(2,1)S(1)} %pad_maximum_fusion.1.refs_0_), channel_id=1, source_target_pairs={{0,1},{1,0},{2,3},{3,2},{4,5},{5,4},{6,7},{7,6},{8,9},{9,8},{10,11... | collective-permute-start | bytes 1769480 | tf_op jit(solution)/shard_map/ppermute | solution.py:366
  67.5 20.9 %collective-permute-start.18 = (bf16[2,9,32,256]{3,2,1,0:T(8,128)(2,1)}, bf16[2,9,32,256]{3,2,1,0:T(8,128)(2,1)}, u32[]{:S(2)}, u32[]{:S(2)}) collective-permute-start(bf16[2,9,32,256]{3,2,1,0:T(8,128)(2,1)} %slice.158), channel_id=1, source_target_pairs={{0,2},{2,0},{1,3},{3,1},{4,6},{6,4},{5,7},{7,5},{8,10},{10,8},{9,1... | collective-permute-start | bytes 884744 | tf_op jit(solution)/shard_map/ppermute | solution.py:366
  68.0 20.7 %collective-permute-start.20 = (bf16[2,9,32,256]{3,2,1,0:T(8,128)(2,1)}, bf16[2,9,32,256]{3,2,1,0:T(8,128)(2,1)}, u32[]{:S(2)}, u32[]{:S(2)}) collective-permute-start(bf16[2,9,32,256]{3,2,1,0:T(8,128)(2,1)} %slice.159), channel_id=1, source_target_pairs={{0,16},{16,0},{1,17},{17,1},{2,18},{18,2},{3,19},{19,3},{4,20},{20... | collective-permute-start | bytes 884744 | tf_op jit(solution)/shard_map/ppermute | solution.py:366
  69.5 24.9 %collective-permute-start.15 = (bf16[4,9,32,256]{3,2,1,0:T(8,128)(2,1)S(1)}, bf16[4,9,32,256]{3,2,1,0:T(8,128)(2,1)S(1)}, u32[]{:S(2)}, u32[]{:S(2)}) collective-permute-start(bf16[4,9,32,256]{3,2,1,0:T(8,128)(2,1)S(1)} %collective-permute-done.14.refs_2_), channel_id=1, source_target_pairs={{0,1},{1,0},{2,3},{3,2},{4,5},{5,4},{6,7},{7,6},{8,9},{9,8},{10,11... | collective-permute-start | bytes 1769480 | tf_op jit(solution)/shard_map/ppermute | solution.py:366
  69.6 24.8 %collective-permute-start.17 = (bf16[4,9,32,256]{3,2,1,0:T(8,128)(2,1)S(1)}, bf16[4,9,32,256]{3,2,1,0:T(8,128)(2,1)S(1)}, u32[]{:S(2)}, u32[]{:S(2)}) collective-permute-start(bf16[4,9,32,256]{3,2,1,0:T(8,128)(2,1)S(1)} %collective-permute-done.16.refs_4_), channel_id=1, source_target_pairs={{0,1},{1,0},{2,3},{3,2},{4,5},{5,4},{6,7},{7,6},{8,9},{9,8},{10,11... | collective-permute-start | bytes 1769480 | tf_op jit(solution)/shard_map/ppermute | solution.py:366
  83.6 15.1 %all-to-all-start = ((f32[32,4,512]{2,1,0:T(4,128)}), f32[32,4,512]{2,1,0:T(4,128)}, u32[]{:S(2)}, u32[]{:S(2)}) async-start(f32[32,4,512]{2,1,0:T(4,128)} %get-tuple-element.35), calls=%async_computation | async-start | bytes 524288 | tf_op jit(solution)/shard_map/all_to_all | solution.py:486
  88.4 6.0 %collective-permute-start.19 = (bf16[2,9,32,256]{3,2,1,0:T(8,128)(2,1)}, bf16[2,9,32,256]{3,2,1,0:T(8,128)(2,1)}, u32[]{:S(2)}, u32[]{:S(2)}) collective-permute-start(bf16[2,9,32,256]{3,2,1,0:T(8,128)(2,1)} %collective-permute-done.18.refs_6_), channel_id=1, source_target_pairs={{0,1},{1,0},{2,3},{3,2},{4,5},{5,4},{6,7},{7,6},{8,9},{9,8},{10,11... | collective-permute-start | bytes 884744 | tf_op jit(solution)/shard_map/ppermute | solution.py:366
  88.7 5.8 %collective-permute-start.21 = (bf16[2,9,32,256]{3,2,1,0:T(8,128)(2,1)}, bf16[2,9,32,256]{3,2,1,0:T(8,128)(2,1)}, u32[]{:S(2)}, u32[]{:S(2)}) collective-permute-start(bf16[2,9,32,256]{3,2,1,0:T(8,128)(2,1)} %collective-permute-done.20.refs_8_), channel_id=1, source_target_pairs={{0,1},{1,0},{2,3},{3,2},{4,5},{5,4},{6,7},{7,6},{8,9},{9,8},{10,11... | collective-permute-start | bytes 884744 | tf_op jit(solution)/shard_map/ppermute | solution.py:366
  94.4 4.3 %copy-start.10 = (bf16[4,9,32,256]{3,2,1,0:T(8,128)(2,1)}, bf16[4,9,32,256]{3,2,1,0:T(8,128)(2,1)S(1)}, u32[]{:S(2)}) copy-start(bf16[4,9,32,256]{3,2,1,0:T(8,128)(2,1)S(1)} %collective-permute-done.13.refs_1_) | copy-start | bytes 1769476
  98.7 10.9 %copy-start.29 = (bf16[6,5,5,512]{3,0,2,1:T(8,128)(2,1)S(1)}, bf16[6,5,5,512]{3,0,2,1:T(8,128)(2,1)}, u32[]{:S(2)}) copy-start(bf16[6,5,5,512]{3,0,2,1:T(8,128)(2,1)} %param.21) | copy-start | bytes 460804
  106.7 13.0 %all-to-all-start.2 = ((f32[32,4,512]{2,1,0:T(4,128)}), f32[32,4,512]{2,1,0:T(4,128)S(1)}, u32[]{:S(2)}, u32[]{:S(2)}) async-start(f32[32,4,512]{2,1,0:T(4,128)} %get-tuple-element.37), calls=%async_computation.2 | async-start | bytes 524288 | tf_op jit(solution)/shard_map/all_to_all | solution.py:486
  138.8 15.4 %all-to-all-start.7 = ((bf16[4,2,64,640]{3,2,1,0:T(8,128)(2,1)}), bf16[4,2,64,640]{3,2,1,0:T(8,128)(2,1)S(1)}, u32[]{:S(2)}, u32[]{:S(2)}) async-start(bf16[4,2,64,640]{3,2,1,0:T(8,128)(2,1)} %bitcast.108), calls=%async_computation.7 | async-start | bytes 1310720 | tf_op jit(solution)/shard_map/all_to_all | solution.py:408
  142.5 23.8 %collective-permute-start.27 = (bf16[544,512]{1,0:T(8,128)(2,1)S(1)}, bf16[544,512]{1,0:T(8,128)(2,1)S(1)}, u32[]{:S(2)}, u32[]{:S(2)}) collective-permute-start(bf16[544,512]{1,0:T(8,128)(2,1)S(1)} %copy-done.18), channel_id=1, source_target_pairs={{0,2},{2,0},{1,3},{3,1},{4,6},{6,4},{5,7},{7,5},{8,10},{10,8},{9,1... | collective-permute-start | bytes 1671176 | tf_op jit(solution)/shard_map/ppermute | solution.py:366
  144.5 21.8 %collective-permute-start.28 = (bf16[544,512]{1,0:T(8,128)(2,1)S(1)}, bf16[544,512]{1,0:T(8,128)(2,1)S(1)}, u32[]{:S(2)}, u32[]{:S(2)}) collective-permute-start(bf16[544,512]{1,0:T(8,128)(2,1)S(1)} %copy-done.18), channel_id=1, source_target_pairs={{0,16},{16,0},{1,17},{17,1},{2,18},{18,2},{3,19},{19,3},{4,20},{20... | collective-permute-start | bytes 1671176 | tf_op jit(solution)/shard_map/ppermute | solution.py:366
  145.9 32.6 %collective-permute-start.29 = (bf16[544,512]{1,0:T(8,128)(2,1)S(1)}, bf16[544,512]{1,0:T(8,128)(2,1)S(1)}, u32[]{:S(2)}, u32[]{:S(2)}) collective-permute-start(bf16[544,512]{1,0:T(8,128)(2,1)S(1)} %copy-done.18), channel_id=1, source_target_pairs={{0,18},{2,16},{16,2},{18,0},{1,19},{3,17},{17,3},{19,1},{4,22},{6,... | collective-permute-start | bytes 1671176 | tf_op jit(solution)/shard_map/ppermute | solution.py:370
  154.2 24.3 %copy-start.9 = (bf16[4,2,64,640]{3,2,1,0:T(8,128)(2,1)}, bf16[4,2,64,640]{3,2,1,0:T(8,128)(2,1)S(1)}, u32[]{:S(2)}) copy-start(bf16[4,2,64,640]{3,2,1,0:T(8,128)(2,1)S(1)} %all-to-all-done.7) | copy-start | bytes 1966084
  154.2 35.6 %all-to-all-start.4 = ((f32[32,2,512]{2,1,0:T(2,128)}), f32[32,2,512]{2,1,0:T(2,128)}, u32[]{:S(2)}, u32[]{:S(2)}) async-start(f32[32,2,512]{2,1,0:T(2,128)} %get-tuple-element.45), calls=%async_computation.4 | async-start | bytes 262144 | tf_op jit(solution)/shard_map/all_to_all | solution.py:486
  166.2 12.3 %copy-start.21 = (bf16[544,512]{1,0:T(8,128)(2,1)}, bf16[544,512]{1,0:T(8,128)(2,1)S(1)}, u32[]{:S(2)}) copy-start(bf16[544,512]{1,0:T(8,128)(2,1)S(1)} %collective-permute-done.27.refs_1_) | copy-start | bytes 1671172
  166.2 12.3 %copy-start.22 = (bf16[544,512]{1,0:T(8,128)(2,1)}, bf16[544,512]{1,0:T(8,128)(2,1)S(1)}, u32[]{:S(2)}) copy-start(bf16[544,512]{1,0:T(8,128)(2,1)S(1)} %collective-permute-done.28.refs_2_) | copy-start | bytes 1671172
  179.4 6.8 %copy-start = (bf16[544,512]{1,0:T(8,128)(2,1)S(1)}, bf16[544,512]{1,0:T(8,128)(2,1)}, u32[]{:S(2)}) copy-start(bf16[544,512]{1,0:T(8,128)(2,1)} %pad_maximum_fusion.3.x_ref.refs_0_) | copy-start | bytes 1671172
  186.3 42.0 %collective-permute-start.30 = (bf16[4,9,16,512]{3,2,1,0:T(8,128)(2,1)}, bf16[4,9,16,512]{3,2,1,0:T(8,128)(2,1)S(1)}, u32[]{:S(2)}, u32[]{:S(2)}) collective-permute-start(bf16[4,9,16,512]{3,2,1,0:T(8,128)(2,1)} %get-tuple-element.53), channel_id=1, source_target_pairs={{0,1},{1,0},{2,3},{3,2},{4,5},{5,4},{6,7},{7,6},{8,9},{9,8},{10,11... | collective-permute-start | bytes 1769480 | tf_op jit(solution)/shard_map/ppermute | solution.py:366
  186.3 15.5 %collective-permute-start.22 = (bf16[544,512]{1,0:T(8,128)(2,1)S(1)}, bf16[544,512]{1,0:T(8,128)(2,1)S(1)}, u32[]{:S(2)}, u32[]{:S(2)}) collective-permute-start(bf16[544,512]{1,0:T(8,128)(2,1)S(1)} %copy-done), channel_id=1, source_target_pairs={{0,2},{2,0},{1,3},{3,1},{4,6},{6,4},{5,7},{7,5},{8,10},{10,8},{9,1... | collective-permute-start | bytes 1671176 | tf_op jit(solution)/shard_map/ppermute | solution.py:366
  186.9 30.9 %collective-permute-start.23 = (bf16[544,512]{1,0:T(8,128)(2,1)S(1)}, bf16[544,512]{1,0:T(8,128)(2,1)S(1)}, u32[]{:S(2)}, u32[]{:S(2)}) collective-permute-start(bf16[544,512]{1,0:T(8,128)(2,1)S(1)} %copy-done), channel_id=1, source_target_pairs={{0,16},{16,0},{1,17},{17,1},{2,18},{18,2},{3,19},{19,3},{4,20},{20... | collective-permute-start | bytes 1671176 | tf_op jit(solution)/shard_map/ppermute | solution.py:366
  187.7 30.2 %collective-permute-start.24 = (bf16[544,512]{1,0:T(8,128)(2,1)S(1)}, bf16[544,512]{1,0:T(8,128)(2,1)}, u32[]{:S(2)}, u32[]{:S(2)}) collective-permute-start(bf16[544,512]{1,0:T(8,128)(2,1)S(1)} %copy-done), channel_id=1, source_target_pairs={{0,18},{2,16},{16,2},{18,0},{1,19},{3,17},{17,3},{19,1},{4,22},{6,... | collective-permute-start | bytes 1671176 | tf_op jit(solution)/shard_map/ppermute | solution.py:370
  192.9 27.7 %all-to-all-start.5 = ((bf16[4,2,64,640]{3,2,1,0:T(8,128)(2,1)}), bf16[4,2,64,640]{3,2,1,0:T(8,128)(2,1)S(1)}, u32[]{:S(2)}, u32[]{:S(2)}) async-start(bf16[4,2,64,640]{3,2,1,0:T(8,128)(2,1)} %bitcast.107), calls=%async_computation.5 | async-start | bytes 1310720 | tf_op jit(solution)/shard_map/all_to_all | solution.py:408
  201.8 18.8 %copy-start.19 = (bf16[544,512]{1,0:T(8,128)(2,1)}, bf16[544,512]{1,0:T(8,128)(2,1)S(1)}, u32[]{:S(2)}) copy-start(bf16[544,512]{1,0:T(8,128)(2,1)S(1)} %collective-permute-done.22.refs_1_) | copy-start | bytes 1671172
  221.4 6.9 %copy-start.13 = (f32[4,9,16,512]{3,2,1,0:T(8,128)S(1)}, f32[4,9,16,512]{3,2,1,0:T(8,128)}, u32[]{:S(2)}) copy-start(f32[4,9,16,512]{3,2,1,0:T(8,128)} %get-tuple-element.52) | copy-start | bytes 3538948
  228.3 16.5 %collective-permute-start.25 = (bf16[4,9,16,512]{3,2,1,0:T(8,128)(2,1)}, bf16[4,9,16,512]{3,2,1,0:T(8,128)(2,1)S(1)}, u32[]{:S(2)}, u32[]{:S(2)}) collective-permute-start(bf16[4,9,16,512]{3,2,1,0:T(8,128)(2,1)} %get-tuple-element.49), channel_id=1, source_target_pairs={{0,1},{1,0},{2,3},{3,2},{4,5},{5,4},{6,7},{7,6},{8,9},{9,8},{10,11... | collective-permute-start | bytes 1769480 | tf_op jit(solution)/shard_map/ppermute | solution.py:366
  229.4 20.4 %all-to-all-start.8 = ((bf16[4,9,16,512]{3,2,1,0:T(8,128)(2,1)}), bf16[4,9,16,512]{3,2,1,0:T(8,128)(2,1)S(1)}, u32[]{:S(2)}, u32[]{:S(2)}) async-start(bf16[4,9,16,512]{3,2,1,0:T(8,128)(2,1)} %add_convert_fusion), calls=%async_computation.8 | async-start | bytes 1179648 | tf_op jit(solution)/shard_map/all_to_all | solution.py:421
  247.1 6.9 %slice-start.1 = ((f32[544,512]{1,0:T(8,128)}), f32[180,512]{1,0:T(8,128)S(1)}, s32[]{:S(2)}) async-start(f32[544,512]{1,0:T(8,128)} %shard_map.244), calls=%async_computation.10 | async-start | bytes 753664 | tf_op jit(solution)/shard_map/slice | solution.py:75
  249.8 19.5 %all-to-all-start.6 = ((bf16[4,9,16,512]{3,2,1,0:T(8,128)(2,1)}), bf16[4,9,16,512]{3,2,1,0:T(8,128)(2,1)S(1)}, u32[]{:S(2)}, u32[]{:S(2)}) async-start(bf16[4,9,16,512]{3,2,1,0:T(8,128)(2,1)} %add_convert_fusion.1), calls=%async_computation.6 | async-start | bytes 1179648 | tf_op jit(solution)/shard_map/all_to_all | solution.py:421
  255.1 15.1 %collective-permute-start.31 = (bf16[9,16,512]{2,1,0:T(8,128)(2,1)S(1)}, bf16[9,16,512]{2,1,0:T(8,128)(2,1)}, u32[]{:S(2)}, u32[]{:S(2)}) collective-permute-start(bf16[9,16,512]{2,1,0:T(8,128)(2,1)S(1)} %reduce_sum.25), channel_id=1, source_target_pairs={{0,16},{16,0},{1,17},{17,1},{2,18},{18,2},{3,19},{19,3},{4,20},{20... | collective-permute-start | bytes 442376 | tf_op jit(solution)/shard_map/ppermute | solution.py:366
  256.7 18.0 %copy-start.3 = (f32[2,3,3,512,32]{3,4,2,1,0:T(8,128)S(1)}, f32[2,3,3,512,32]{3,4,2,1,0:T(8,128)}, u32[]{:S(2)}) copy-start(f32[2,3,3,512,32]{3,4,2,1,0:T(8,128)} %param.24) | copy-start | bytes 3538948
  256.7 18.0 %copy-start.14 = (f32[2,3,3,512,32]{3,4,2,1,0:T(8,128)S(1)}, f32[2,3,3,512,32]{3,4,2,1,0:T(8,128)}, u32[]{:S(2)}) copy-start(f32[2,3,3,512,32]{3,4,2,1,0:T(8,128)} %param.27) | copy-start | bytes 3538948
  269.4 5.2 %collective-permute-start.26 = (bf16[9,16,512]{2,1,0:T(8,128)(2,1)S(1)}, bf16[9,16,512]{2,1,0:T(8,128)(2,1)S(1)}, u32[]{:S(2)}, u32[]{:S(2)}) collective-permute-start(bf16[9,16,512]{2,1,0:T(8,128)(2,1)S(1)} %reduce_sum.24), channel_id=1, source_target_pairs={{0,16},{16,0},{1,17},{17,1},{2,18},{18,2},{3,19},{19,3},{4,20},{20... | collective-permute-start | bytes 442376 | tf_op jit(solution)/shard_map/ppermute | solution.py:366
  (20 other events, 46.6 us)
